TPU v7x, 256 devices: a whole 4x4x8 slice. The times are simulated.
256 devices in a mesh: dp: 4 (over x), seq: 64 (over y, z, core).
Axes of the slice: x: 4, y: 4, z: 8, core: 2. Of those that a mesh axis runs over, the one named last changes fastest.
Arguments:
- queries: bfloat16 [4, 8192, 4096], P('dp', 'seq'), may hold values from -120 to 120
- encoded: bfloat16 [4, 64, 12, 128, 896], P('dp', 'seq'), may hold values from -8 to 8
- projection: bfloat16 [896, 8192], P(None, ('dp', 'seq')), may hold values from -0.1875 to 0.1875
- neighbour_shard: int32 [4, 128, 2], P('dp', 'seq'), may hold values from 0 to 3, all different within a row; in each aligned block of 2 rows (0 to 1, 2 to 3, ..., all dimensions but the last counted through in order) at most 2 rows name the same one
- neighbour_block: int32 [4, 128, 2], P('dp', 'seq'), may hold values from 0 to 11
Outputs:
- attended: bfloat16 [4, 8192, 4096], P('dp', 'seq')
Inputs may be any that keep to these rules, and one draw needn't show every extreme that they name: `neighbour_shard`: each span's 2 neighbours lie in different shards; among the 2 spans of one device no shard is named more than 2 times, and some device names one shard 2 times.
All inputs are finite; a program needn't handle non-finite values.
Results may differ from a plain program's by a relative error of at most 0.0062.
Values may be sent and summed in bfloat16 or wider, within the bound.
A program may use at most 128 MiB of HBM per device.

v0:
```python
import math

import jax
import jax.numpy as jnp
from jax import lax
from jax.sharding import PartitionSpec as P

HD = 128
CH = 64


def passed_along(value, axis, steps):
    count = lax.axis_size(axis)
    initial, last = (max(0, -steps), min(count, count - steps))
    return lax.ppermute(value, axis, [(source, source + steps) for source in range(initial, last)])


def attend_blocks(span_rows, key_value):
    blocks = span_rows.shape[0]
    groups = span_rows.shape[2] // HD
    query_split = span_rows.reshape(blocks, span_rows.shape[1], groups, HD)
    head_split = key_value.reshape(blocks, key_value.shape[1], groups, 2, HD)
    scores = jnp.einsum(
        "cihd,cjhd->chij", query_split, head_split[:, :, :, 0], preferred_element_type=jnp.float32
    )
    scores = scores * (1.0 / math.sqrt(HD))
    weights = jax.nn.softmax(scores, axis=-1).astype(jnp.bfloat16)
    combined = jnp.einsum(
        "chij,cjhd->cihd", weights, head_split[:, :, :, 1], preferred_element_type=jnp.float32
    )
    return combined.astype(jnp.bfloat16).reshape(blocks * span_rows.shape[1], groups * HD)


def project(tokens, segment):
    return jnp.dot(tokens, segment, preferred_element_type=jnp.float32).astype(jnp.bfloat16)


def body(queries, encoded, projection, neighbour_shard, neighbour_block):
    shards = lax.axis_size("dp")
    myself = lax.axis_index("dp")
    spans = neighbour_shard.shape[1]
    neighbours = neighbour_shard.shape[2]
    requests = spans * neighbours
    length = encoded.shape[3]
    enc_width = encoded.shape[4]
    every_shard, every_block = (
        lax.all_gather(neighbour_shard, "dp", axis=0, tiled=True),
        lax.all_gather(neighbour_block, "dp", axis=0, tiled=True),
    )
    every_shard = every_shard.reshape(shards, requests)
    every_block = every_block.reshape(shards, requests)
    wanted = every_shard == myself
    ranking = jnp.cumsum(wanted.astype(jnp.int32), axis=1) - 1
    places = jnp.arange(spans, dtype=jnp.int32)
    chosen = wanted[:, None, :] & (ranking[:, None, :] == places[None, :, None])
    source_rows = jnp.sum(jnp.where(chosen, every_block[:, None, :], 0), axis=2)
    filled = jnp.any(chosen, axis=2)
    packed = jnp.take(encoded[0, 0], source_rows.reshape(-1), axis=0)
    packed = packed.reshape(shards, spans, length, enc_width)
    packed = jnp.where(filled[:, :, None, None], packed, jnp.zeros((), packed.dtype))
    received = lax.all_to_all(packed, "dp", split_axis=0, concat_axis=0, tiled=True)
    own_shard = neighbour_shard.reshape(requests)
    earlier = jnp.arange(requests)[None, :] < jnp.arange(requests)[:, None]
    same_shard = own_shard[None, :] == own_shard[:, None]
    own_rank = jnp.sum((earlier & same_shard).astype(jnp.int32), axis=1)
    lookup = own_shard * spans + own_rank
    arrived = jnp.take(received.reshape(shards * spans, length, enc_width), lookup, axis=0)
    local_rows = queries[0]
    incoming = passed_along(local_rows[: CH - 1], "seq", -1)
    attending = jnp.concatenate([local_rows[CH - 1 :], incoming], axis=0)
    tokens = arrived.reshape(requests * length, enc_width)
    key_value = project(tokens, lax.all_gather(projection, ("dp", "seq"), axis=1, tiled=True))
    combined = attend_blocks(
        attending.reshape(spans, CH, -1), key_value.reshape(spans, neighbours * length, -1)
    )
    row_total = combined.shape[0]
    outgoing = passed_along(combined[row_total - (CH - 1) :], "seq", 1)
    result = jnp.concatenate([outgoing, combined[: row_total - (CH - 1)]], axis=0)
    return result[None]


def solution(mesh):
    placed = (
        P("dp", "seq", None),
        P("dp", "seq", None, None, None),
        P(None, ("dp", "seq")),
        P("dp", "seq", None),
        P("dp", "seq", None),
    )
    return jax.shard_map(
        body, mesh=mesh, in_specs=placed, out_specs=P("dp", "seq", None), check_vma=False
    )
```

profile of v0, /device:TPU:8, one launch (start us, length us, event | category | flops | bytes accessed | tf_op | source)
XLA Modules:
  0.0 232.8 jit_solution(14708834216003925928)
XLA Ops:
  6.5 0.7 all-gather.2.cloned.1.call-update
  7.3 10.1 %all_gather.9 = s32[4,2,2]{2,1,0:T(2,128)S(1)} all-gather(s32[1,2,2]{2,1,0:T(2,128)} %param.8), channel_id=1, replica_groups=mesh['dp'=4,'seq'=64] {'dp'}, dimensions={0}, use_global_device_ids=true | all-gather | bytes 80 | tf_op jit(solution)/shard_map/all_gather | solution.py:47
  17.4 7.3 %all_gather.10 = s32[4,2,2]{2,1,0:T(2,128)S(1)} all-gather(s32[1,2,2]{2,1,0:T(2,128)} %param.9), channel_id=1, replica_groups=mesh['dp'=4,'seq'=64] {'dp'}, dimensions={0}, use_global_device_ids=true | all-gather | bytes 80 | tf_op jit(solution)/shard_map/all_gather | solution.py:48
  25.2 0.1 select_reduce_fusion
  25.7 0.2 fusion.16
  25.8 0.1 copy.46
  26.0 2.0 gather_fusion
  28.0 3.1 %select_select_fusion = bf16[4,2,128,896]{3,2,1,0:T(8,128)(2,1)} fusion(bf16[4,2,128,896]{3,2,1,0:T(8,128)(2,1)} %bitcast.48, pred[4,2]{1,0:T(4,128)(4,1)S(1)} %copy.49, pred[4,2]{1,0:T(4,128)(4,1)S(1)} %copy.46), kind=kLoop, calls=%fused_computation.14 | loop fusion | flops 1835008 | bytes 3670032 | tf_op jit(solution)/shard_map/jit(_where)/select_n | solution.py:60
  31.1 4.4 %all-to-all-start = ((bf16[4,2,128,896]{3,2,1,0:T(8,128)(2,1)}), bf16[4,2,128,896]{3,2,1,0:T(8,128)(2,1)}, u32[]{:S(2)}, u32[]{:S(2)}) async-start(bf16[4,2,128,896]{3,2,1,0:T(8,128)(2,1)} %select_select_fusion), calls=%async_computation | async-start | bytes 3670016 | tf_op jit(solution)/shard_map/all_to_all | solution.py:61
  35.6 3.4 %collective-permute-start = (bf16[63,4096]{1,0:T(8,128)(2,1)S(1)}, bf16[63,4096]{1,0:T(8,128)(2,1)S(1)}, u32[]{:S(2)}, u32[]{:S(2)}) collective-permute-start(bf16[63,4096]{1,0:T(8,128)(2,1)S(1)} %slice_bitcast_fusion.1), channel_id=1, source_target_pairs={{1,0},{2,1},{3,2},{4,3},{5,4},{6,5},{7,6},{8,7},{9,8},{10,9},{11,1... | collective-permute-start | bytes 1548296 | tf_op jit(solution)/shard_map/ppermute | solution.py:15
  39.1 0.2 convert_reduce_fusion
  39.3 0.1 slice_bitcast_fusion
  39.6 6.5 %collective-permute-done = bf16[63,4096]{1,0:T(8,128)(2,1)S(1)} collective-permute-done((bf16[63,4096]{1,0:T(8,128)(2,1)S(1)}, bf16[63,4096]{1,0:T(8,128)(2,1)S(1)}, u32[]{:S(2)}, u32[]{:S(2)}) %collective-permute-start) | collective-permute-done | bytes 516128 | tf_op jit(solution)/shard_map/ppermute | solution.py:15
  46.0 0.2 maximum_bitcast_fusion
  46.2 0.2 copy.57
  46.5 9.4 %all-to-all-done = bf16[4,2,128,896]{3,2,1,0:T(8,128)(2,1)} async-done(((bf16[4,2,128,896]{3,2,1,0:T(8,128)(2,1)}), bf16[4,2,128,896]{3,2,1,0:T(8,128)(2,1)}, u32[]{:S(2)}, u32[]{:S(2)}) %all-to-all-start) | async-done | bytes 1835040 | tf_op jit(solution)/shard_map/all_to_all | solution.py:61
  55.9 2.2 gather_fusion.1
  58.1 1.1 bitcast_select_fusion
  59.3 77.8 %all-gather.2.cloned.1.call-done = bf16[896,8192]{0,1:T(8,128)(2,1)} async-done(((bf16[896,32]{0,1:T(8,128)(2,1)}), bf16[896,8192]{0,1:T(8,128)(2,1)}) %all-gather.2.cloned.1.call-update) | async-done | bytes 14680080 | tf_op jit(solution)/shard_map/all_gather | solution.py:72
  137.1 14.4 %convolution_convert_fusion = bf16[512,8192]{1,0:T(8,128)(2,1)} fusion(bf16[512,896]{1,0:T(8,128)(2,1)} %bitcast_select_fusion, bf16[896,8192]{0,1:T(8,128)(2,1)} %all-gather.2.cloned.1.call-done), kind=kOutput, calls=%fused_computation.3 | convolution fusion | flops 7520387072 | bytes 23986176 | tf_op jit(solution)/shard_map/dot_general | solution.py:35
  151.5 14.3 %reshape_reshape.6 = bf16[2,256,32,2,128]{4,3,2,1,0:T(2,128)(2,1)} reshape(bf16[512,8192]{1,0:T(8,128)(2,1)} %convolution_convert_fusion) | data formatting | bytes 16777216 | tf_op jit(solution)/shard_map/reshape;reshape | solution.py:22
  165.7 19.4 %fusion.24 = (bf16[2,256,32,1,128]{4,3,2,1,0:T(2,128)(2,1)S(1)}, bf16[2,256,32,1,128]{4,3,2,1,0:T(2,128)(2,1)}) fusion(bf16[2,256,32,2,128]{4,3,2,1,0:T(2,128)(2,1)} %reshape_reshape.6), kind=kLoop, calls=%fused_computation.49 | loop fusion | bytes 16777216 | tf_op jit(solution)/shard_map/slice | solution.py:24
  185.1 4.9 %fusion.2 = f32[2,32,64,256]{3,2,1,0:T(8,128)S(1)} fusion(bf16[2,256,32,1,128]{4,3,2,1,0:T(2,128)(2,1)S(1)} %get-tuple-element.5, bf16[2,64,32,128]{3,2,1,0:T(8,128)(2,1)S(1)} %bitcast.51), kind=kOutput, calls=%fused_computation.7 | convolution fusion | flops 268435456 | bytes 9437184 | tf_op jit(solution)/shard_map/cihd,cjhd->chij/dot_general | solution.py:23
  190.0 1.9 copy-done.2
  191.9 1.6 fusion.25
  193.5 16.1 %fusion.9 = bf16[2,64,32,128]{3,1,2,0:T(8,128)(2,1)} fusion(bf16[2,256,32,1,128]{4,3,2,1,0:T(2,128)(2,1)} %get-tuple-element.6, f32[2,32,64]{2,1,0:T(8,128)S(1)} %fusion.25, f32[2,32,64,256]{3,2,1,0:T(8,128)} %copy-done.2), kind=kOutput, calls=%fused_computation.16 | convolution fusion | flops 274206976 | bytes 9453568 | tf_op jit(solution)/shard_map/chij,cjhd->cihd/dot_general | solution.py:28
  209.7 1.9 copy.54
  211.6 0.5 copy.70
  212.1 0.1 slice.38
  212.2 2.2 collective-permute-start.1
  214.4 10.4 %collective-permute-done.1 = bf16[63,4096]{1,0:T(8,128)(2,1)S(1)} collective-permute-done((bf16[63,4096]{1,0:T(8,128)(2,1)S(1)}, bf16[63,4096]{1,0:T(8,128)(2,1)S(1)}, u32[]{:S(2)}, u32[]{:S(2)}) %collective-permute-start.1) | collective-permute-done | bytes 516128 | tf_op jit(solution)/shard_map/ppermute | solution.py:15
  224.8 1.1 maximum_bitcast_fusion.1
  (35 shorter events, 1.2 us)
Async XLA Ops:
  6.5 19.4 %copy-start = (bf16[1,1,12,128,896]{4,3,2,1,0:T(8,128)(2,1)S(1)}, bf16[1,1,12,128,896]{4,3,2,1,0:T(8,128)(2,1)}, u32[]{:S(2)}) copy-start(bf16[1,1,12,128,896]{4,3,2,1,0:T(8,128)(2,1)} %param.6) | copy-start | bytes 8257540
  6.5 130.6 %all-gather.2.cloned.1.call-start = ((), (), s32[]{:S(2)}) async-start(), calls=%async_computation.1 | async-start | bytes 14737408 | tf_op jit(solution)/shard_map/all_gather | solution.py:72
  28.0 7.6 %copy-start.3 = (bf16[1,128,4096]{2,1,0:T(8,128)(2,1)S(1)}, bf16[1,128,4096]{2,1,0:T(8,128)(2,1)}, u32[]{:S(2)}) copy-start(bf16[1,128,4096]{2,1,0:T(8,128)(2,1)} %param.5) | copy-start | bytes 3145732
  28.0 11.0 %copy-start.4 = (s32[1,2,2]{2,1,0:T(2,128)S(1)}, s32[1,2,2]{2,1,0:T(2,128)}, u32[]{:S(2)}) copy-start(s32[1,2,2]{2,1,0:T(2,128)} %param.8) | copy-start | bytes 52
  31.1 24.8 %all-to-all-start = ((bf16[4,2,128,896]{3,2,1,0:T(8,128)(2,1)}), bf16[4,2,128,896]{3,2,1,0:T(8,128)(2,1)}, u32[]{:S(2)}, u32[]{:S(2)}) async-start(bf16[4,2,128,896]{3,2,1,0:T(8,128)(2,1)} %select_select_fusion), calls=%async_computation | async-start | bytes 3670016 | tf_op jit(solution)/shard_map/all_to_all | solution.py:61
  35.6 10.5 %collective-permute-start = (bf16[63,4096]{1,0:T(8,128)(2,1)S(1)}, bf16[63,4096]{1,0:T(8,128)(2,1)S(1)}, u32[]{:S(2)}, u32[]{:S(2)}) collective-permute-start(bf16[63,4096]{1,0:T(8,128)(2,1)S(1)} %slice_bitcast_fusion.1), channel_id=1, source_target_pairs={{1,0},{2,1},{3,2},{4,3},{5,4},{6,5},{7,6},{8,7},{9,8},{10,9},{11,1... | collective-permute-start | bytes 1548296 | tf_op jit(solution)/shard_map/ppermute | solution.py:15
  190.0 1.9 copy-start.2
  193.5 32.4 %copy-start.1 = (bf16[1,1,12,128,896]{4,3,2,1,0:T(8,128)(2,1)S(1)}, bf16[1,1,12,128,896]{4,3,2,1,0:T(8,128)(2,1)}, u32[]{:S(2)}) copy-start(bf16[1,1,12,128,896]{4,3,2,1,0:T(8,128)(2,1)} %param.6) | copy-start | bytes 8257540
  212.2 12.6 %collective-permute-start.1 = (bf16[63,4096]{1,0:T(8,128)(2,1)S(1)}, bf16[63,4096]{1,0:T(8,128)(2,1)S(1)}, u32[]{:S(2)}, u32[]{:S(2)}) collective-permute-start(bf16[63,4096]{1,0:T(8,128)(2,1)S(1)} %slice.38), channel_id=1, source_target_pairs={{0,1},{1,2},{2,3},{3,4},{4,5},{5,6},{6,7},{7,8},{8,9},{9,10},{10,1... | collective-permute-start | bytes 1548296 | tf_op jit(solution)/shard_map/ppermute | solution.py:15
Sparse Core Ops, SparseCore 0:
  10.9 126.1 all-gather.1
where the time goes:
time: 234 us; the launch traced here: 233 us
  waiting for transfers between devices  105 us (45%)
  local copies, waits for them, and re-layouts  43.9 us (19%)
  matrix products  35.4 us (15%)
  blocking collectives  17.4 us (7%)
  between operations  13.6 us (6%)
  starting transfers between devices  9.93 us (4%)
  other arithmetic  7.76 us (3%)
    all_gather x1, waiting for transfers between devices, body(): lax.all_gather(projection, ('dp', 'seq'), axis=1, tiled=True)  77.8 us
    slice x1, local copies, waits for them, and re-layouts, attend_blocks(): head_split[:, :, :, 0]  19.4 us
    ppermute x2, waiting for transfers between devices, passed_along(): lax.ppermute(value, axis, [(source, source + steps) for source in range(i...  16.9 us
    dot_general x1, matrix products, attend_blocks(): jnp.einsum('chij,cjhd->cihd', weights, head_split[:, :, :, 1], preferred_...  16.1 us
    dot_general x1, matrix products, project(): jnp.dot(tokens, segment, preferred_element_type=jnp.float32)  14.4 us
    another operation x1, local copies, waits for them, and re-layouts, attend_blocks(): head_split = key_value.reshape(blocks, key_value.shape[1], groups, 2, HD)  14.3 us
    all_gather x1, blocking collectives, body(): lax.all_gather(neighbour_shard, 'dp', axis=0, tiled=True)  10.1 us
    all_to_all x1, waiting for transfers between devices, body(): lax.all_to_all(packed, 'dp', split_axis=0, concat_axis=0, tiled=True)  9.43 us
  transfers between devices with their start and end apart: 4, of which 4 were waited for; matrix products, arithmetic and copies ran while one was open for 5% of the time, Pallas kernels for 0%

commit v1 on v0

v1 whole, which is shorter than its diff:
```python
import math

import jax
import jax.numpy as jnp
from jax import lax
from jax.experimental import pallas as pl
from jax.experimental.pallas import tpu as pltpu
from jax.sharding import PartitionSpec as P

MESH = pl.DeviceIdType.MESH
HD = 128
CH = 64
LA = 384
LB = 512
SCALE = 1.0 / math.sqrt(HD)


def dot_nt(a, b):
    return lax.dot_general(a, b, (((1,), (1,)), ((), ())), preferred_element_type=jnp.float32)


def dot_nn(a, b):
    return lax.dot_general(a, b, (((1,), (0,)), ((), ())), preferred_element_type=jnp.float32)


def kernel(
    q_ref, enc_hbm, wt_ref, sh_ref, bl_ref, out_ref,
    WA, WB, enc, packA, packB, recvA, recvB, tokA, tokB, q_all, qs, stage, fix, idx_out, idx_in, idx_smem,
    lsem, ssem, qsem, osem, s_idx, s_tok, s_sib, s_p1x, s_p2z, s_p1y, s_p1z, s_p2x, s_p2y, s_q, s_o,
):
    x = lax.axis_index("dp")
    s = lax.axis_index("seq")
    y = lax.div(s, 16)
    z = lax.rem(lax.div(s, 2), 8)
    k = lax.rem(s, 2)
    yy = lax.div(y, 2)
    cs = lax.rem(y, 2)
    act = cs == k

    def dev(dx=0, dy=0, dz=0, core=None):
        core = k if core is None else core
        return (
            lax.rem(x + dx + 4, 4),
            lax.rem(y + dy + 4, 4) * 16 + lax.rem(z + dz + 8, 8) * 2 + core,
        )

    def chip_along(step, core):
        return (x, lax.rem(lax.div(s, 2) + step + 32, 32) * 2 + core)

    sib = dev(core=1 - k)
    counter = [0]

    def remote(src, dst, rsem, to):
        n = counter[0]
        counter[0] += 1

        def build():
            return pltpu.make_async_remote_copy(
                src_ref=src, dst_ref=dst, send_sem=ssem.at[n], recv_sem=rsem, device_id=to, device_id_type=MESH
            )

        return build

    def arrived(dst, rsem):
        pltpu.make_async_copy(dst, dst, rsem).wait()

    enc_cp = pltpu.make_async_copy(enc_hbm, enc, lsem.at[0])
    enc_cp.start()

    barrier = pltpu.get_barrier_semaphore()
    partners = [sib]
    for c in (0, 1):
        partners += [dev(dx=d, core=c) for d in (1, 2, 3)]
        partners += [dev(dz=d, core=c) for d in range(1, 8)]
        partners += [chip_along(1, c), chip_along(-1, c)]
    partners += [dev(dy=d) for d in (1, 2, 3)]
    for p in partners:
        pl.semaphore_signal(barrier, inc=1, device_id=p, device_id_type=MESH)

    lane = lax.broadcasted_iota(jnp.int32, (8, 128), 1)
    own_sh = [sh_ref[0, e // 2, e % 2] for e in range(4)]
    own_bl = [bl_ref[0, e // 2, e % 2] for e in range(4)]
    codes = jnp.zeros((8, 128), jnp.int32)
    for e in range(4):
        codes = jnp.where(lane == e, own_sh[e], codes)
        codes = jnp.where(lane == 4 + e, own_bl[e], codes)
    idx_out[...] = codes
    pl.semaphore_wait(barrier, len(partners))

    always, if_act, if_pas = [], [], []

    for d in (1, 2, 3):
        always.append(remote(idx_out, idx_in.at[x], s_idx.at[d], dev(dx=d)))
        always[-1]().start()

    wa = wt_ref.at[:, pl.ds(0, LA)]
    wb = wt_ref.at[:, pl.ds(LA, LB)]
    half = pl.ds(pl.multiple_of(k * 32, 32), 32)
    other = pl.ds(pl.multiple_of((1 - k) * 32, 32), 32)
    ownA = lambda: pltpu.make_async_copy(wa, WA.at[x, yy, z, half], lsem.at[1])
    ownB = lambda: pltpu.make_async_copy(wb, WB.at[x, yy, z, half], lsem.at[2])
    sibA = remote(wa, WA.at[x, yy, z, half], s_p1x.at[0, k], sib)
    sibB = remote(wb, WB.at[x, yy, z, half], s_p2z.at[0, k], sib)
    if_pas += [sibA, sibB]

    @pl.when(act)
    def _():
        ownA().start()
        ownB().start()

    @pl.when(jnp.logical_not(act))
    def _():
        sibA().start()
        sibB().start()

    for d in (4, 3, 5, 2, 6, 1, 7):
        always.append(remote(wb, WB.at[x, yy, z, half], s_p2z.at[d, k], dev(dz=d, core=cs)))
        always[-1]().start()
    for d in (2, 1, 3):
        always.append(remote(wa, WA.at[x, yy, z, half], s_p1x.at[d, k], dev(dx=d, core=cs)))
        always[-1]().start()

    enc_cp.wait()
    for d in (1, 2, 3):
        src = lax.rem(x + d, 4)
        arrived(idx_in.at[src], s_idx.at[4 - d])
        cp = pltpu.make_async_copy(idx_in.at[src], idx_smem.at[src], lsem.at[3])
        cp.start()
        cp.wait()

    def wanted(sh, bl):
        m = [v == x for v in sh]
        first = jnp.where(m[0], bl[0], jnp.where(m[1], bl[1], jnp.where(m[2], bl[2], bl[3])))
        last = jnp.where(m[3], bl[3], jnp.where(m[2], bl[2], jnp.where(m[1], bl[1], bl[0])))
        return first, last

    tokB_sends = []
    for d in (2, 1, 3):
        src = lax.rem(x + d, 4)
        pair = wanted([idx_smem[src, 0, e] for e in range(4)], [idx_smem[src, 0, 4 + e] for e in range(4)])
        for i in range(2):
            block = enc[pair[i]]
            packA[d - 1, i] = block[:, :LA]
            packB[d - 1, i] = block[:, LA:]
        mine = pl.ds(x * 2, 2)
        always.append(remote(packA.at[d - 1], recvA.at[mine], s_tok.at[0, d], dev(dx=d)))
        always[-1]().start()
        tokB_sends.append(remote(packB.at[d - 1], recvB.at[mine], s_tok.at[1, d], dev(dx=d)))
    for t in tokB_sends:
        always.append(t)
        t().start()
    pair = wanted(own_sh, own_bl)
    for i in range(2):
        block = enc[pair[i]]
        recvA[x * 2 + i] = block[:, :LA]
        recvB[x * 2 + i] = block[:, LA:]

    p1y = [remote(WA.at[:, yy, z], WA.at[:, yy, z], s_p1y.at[yy], dev(dy=d)) for d in (1, 3, 2)]
    if_act += p1y

    def zstep(direction, step, part):
        plane = lax.rem(z + (8 - (step - 1) if direction == 0 else step - 1), 8)
        return remote(
            WA.at[:, part, plane], WA.at[:, part, plane], s_p1z.at[direction, step - 1, part],
            dev(dz=1 if direction == 0 else -1),
        )

    def zwait(direction, step, part):
        plane = lax.rem(z + (8 - step if direction == 0 else step), 8)
        arrived(WA.at[:, part, plane], s_p1z.at[direction, step - 1, part])

    z_own = [zstep(i, 1, yy) for i in (0, 1)]
    z_far = [zstep(i, 1, 1 - yy) for i in (0, 1)]
    always += z_own + z_far

    p2x = {d: remote(WB.at[x, yy], WB.at[x, yy], s_p2x.at[d], dev(dx=d)) for d in (1, 3, 2)}
    if_act += list(p2x.values())

    def ysend(direction, d, zh, part):
        ref = WB.at[lax.rem(x + d, 4), part, pl.ds(4 * zh, 4)]
        return remote(ref, ref, s_p2y.at[direction, d, zh], dev(dy=1 if direction == 0 else -1))

    def ywait(direction, d, zh):
        part = lax.div(lax.rem(y + (3 if direction == 0 else 1), 4), 2)
        part = jnp.where(act, 1 - yy, part)
        arrived(WB.at[lax.rem(x + d, 4), part, pl.ds(4 * zh, 4)], s_p2y.at[direction, d, zh])

    y_act = {d: [ysend(0, d, 0, yy), ysend(1, d, 1, yy), ysend(0, d, 1, yy), ysend(1, d, 0, yy)] for d in range(4)}
    below, above = lax.div(lax.rem(y + 3, 4), 2), lax.div(lax.rem(y + 1, 4), 2)
    y_pas = {d: [ysend(0, d, 0, below), ysend(1, d, 1, above)] for d in range(4)}
    for d in range(4):
        if_act += y_act[d]
        if_pas += y_pas[d]

    @pl.when(act)
    def _():
        ownA().wait()
        arrived(WA.at[x, yy, z, other], s_p1x.at[0, 1 - k])
        for d in (1, 2, 3):
            for c in (0, 1):
                arrived(WA.at[lax.rem(x + 4 - d, 4), yy, z, pl.ds(c * 32, 32)], s_p1x.at[d, c])
        for t in p1y + z_own:
            t().start()
        ownB().wait()
        arrived(WB.at[x, yy, z, other], s_p2z.at[0, 1 - k])
        for d in range(1, 8):
            for c in (0, 1):
                arrived(WB.at[x, yy, lax.rem(z + 8 - d, 8), pl.ds(c * 32, 32)], s_p2z.at[d, c])
        for t in [p2x[1], p2x[3]] + y_act[0]:
            t().start()
        arrived(WA.at[:, 1 - yy, z], s_p1y.at[1 - yy])
        for t in z_far:
            t().start()

    @pl.when(jnp.logical_not(act))
    def _():
        for part in (0, 1):
            arrived(WA.at[:, part, z], s_p1y.at[part])
        for t in z_own + z_far:
            t().start()

    local_rows = pl.ds(pl.multiple_of(k * 128, 128), 128)

    def qcols(g, core):
        return pl.ds(pl.multiple_of(g * 512 + core * 256, 256), 256)

    def gcols(g):
        return pl.ds(pl.multiple_of(g * 256, 256), 256)

    def q_copies(g):
        loc = pltpu.make_async_copy(q_ref.at[:, qcols(g, k)], q_all.at[local_rows, gcols(g)], lsem.at[4])
        to_sib = pltpu.make_async_remote_copy(
            src_ref=q_ref.at[:, qcols(g, 1 - k)], dst_ref=q_all.at[local_rows, gcols(g)],
            send_sem=qsem.at[0], recv_sem=s_q.at[0], device_id=sib, device_id_type=MESH,
        )
        back = [
            pltpu.make_async_remote_copy(
                src_ref=q_ref.at[pl.ds(0, 64), qcols(g, c)], dst_ref=q_all.at[pl.ds(256, 64), gcols(g)],
                send_sem=qsem.at[1 + c], recv_sem=s_q.at[1], device_id=chip_along(-1, c), device_id_type=MESH,
            )
            for c in (0, 1)
        ]
        return loc, to_sib, back

    @pl.loop(0, 8)
    def _(g):
        loc, to_sib, back = q_copies(g)
        loc.start()
        to_sib.start()

        @pl.when(k == 0)
        def _():
            back[0].start()
            back[1].start()

    z_next = {st: [zstep(i, st, p) for i in (0, 1) for p in (0, 1)] for st in (2, 3)}
    z_last = [zstep(0, 4, 0), zstep(1, 4, 1)]
    for st in (2, 3):
        always += z_next[st]
    always += z_last

    def z_forward(st):
        n = 0
        for i in (0, 1):
            for p in (0, 1):
                zwait(i, st - 1, p)
                if st < 4:
                    z_next[st][n]().start()
                elif i == p:
                    z_last[i]().start()
                n += 1

    def y_forward(d):
        for first in (0, 1):
            ywait(0, d, first)
            ywait(1, d, 1 - first)
            if first == 0:
                y_pas[d][0]().start()
                y_pas[d][1]().start()

    @pl.when(jnp.logical_not(act))
    def _():
        y_forward(0)

    z_forward(2)

    @pl.when(act)
    def _():
        for d in (1, 3):
            arrived(WB.at[lax.rem(x + 4 - d, 4), yy], s_p2x.at[d])
            for t in y_act[4 - d]:
                t().start()
        p2x[2]().start()

    @pl.when(jnp.logical_not(act))
    def _():
        y_forward(3)

    z_forward(3)

    half_tok = []
    rank = [jnp.int32(0)]
    for e in range(1, 4):
        same = own_sh[e] == own_sh[0]
        for f in range(1, e):
            same = jnp.logical_or(same, own_sh[e] == own_sh[f])
        rank.append(jnp.where(same, 1, 0))
    for which, (recv, tok) in enumerate(((recvA, tokA), (recvB, tokB))):
        for d in (1, 2, 3):
            arrived(recv.at[pl.ds(lax.rem(x + 4 - d, 4) * 2, 2)], s_tok.at[which, d])
        for e in range(4):
            tok[k, pl.ds(e * 128, 128)] = recv[own_sh[e] * 2 + rank[e]]
        half_tok.append(remote(tok.at[k], tok.at[k], s_sib.at[which], sib))
        half_tok[-1]().start()
    always += half_tok

    @pl.when(act)
    def _():
        arrived(WB.at[lax.rem(x + 2, 4), yy], s_p2x.at[2])
        for t in y_act[2]:
            t().start()

    @pl.when(jnp.logical_not(act))
    def _():
        y_forward(1)
        y_forward(2)

    z_forward(4)

    whole_q = q_all.at[pl.ds(0, 128)]
    pltpu.make_async_copy(q_ref.at[:, pl.ds(0, 2048)], whole_q, lsem.at[4]).wait()
    arrived(whole_q, s_q.at[0])
    arrived(q_all.at[pl.ds(256, 64)], s_q.at[1])

    @pl.loop(0, 8)
    def _(g):
        rows = q_all[pl.ds(48, 272), gcols(g)].astype(jnp.float32)
        qs[:, gcols(g)] = pltpu.roll(rows, 1, 0)[16:].astype(jnp.bfloat16)

    for which, tok in enumerate((tokA, tokB)):
        arrived(tok.at[1 - k], s_sib.at[which])
    zwait(0, 4, 0)
    zwait(1, 4, 1)

    @pl.when(act)
    def _():
        for d in range(4):
            ywait(0, d, 0)
            ywait(1, d, 1)

    def out_copies(g):
        cols = qcols(g, k)
        mids = pl.ds(pl.multiple_of((1 - k) * 64, 64), 128)
        to_next = pltpu.make_async_remote_copy(
            src_ref=stage.at[g, pl.ds(192, 64)], dst_ref=out_ref.at[pl.ds(0, 64), cols],
            send_sem=osem.at[0], recv_sem=s_o.at[k], device_id=chip_along(1, 0), device_id_type=MESH,
        )
        del mids
        zero = pltpu.make_async_remote_copy(
            src_ref=stage.at[g, pl.ds(64, 128)], dst_ref=out_ref.at[:, cols],
            send_sem=osem.at[1], recv_sem=s_o.at[2], device_id=sib, device_id_type=MESH,
        )
        one = pltpu.make_async_remote_copy(
            src_ref=stage.at[g, pl.ds(0, 64)], dst_ref=out_ref.at[pl.ds(64, 64), cols],
            send_sem=osem.at[2], recv_sem=s_o.at[3], device_id=sib, device_id_type=MESH,
        )
        edge = pltpu.make_async_remote_copy(
            src_ref=stage.at[g, pl.ds(240, 16)], dst_ref=fix.at[:, cols],
            send_sem=osem.at[3], recv_sem=s_o.at[4], device_id=sib, device_id_type=MESH,
        )
        return to_next, zero, one, edge

    @pl.loop(0, 8)
    def _(g):
        xg, yg = lax.div(g, 2), lax.rem(g, 2)
        for zh in (0, 1):
            wa_h = WA[xg, yg, pl.ds(4 * zh, 4)].reshape(256, LA)
            wb_h = WB[xg, yg, pl.ds(4 * zh, 4)].reshape(256, LB)
            cols = pl.ds(pl.multiple_of(g * 256 + zh * 128, 128), 128)
            parts = []
            for j in range(4):
                rows = pl.ds((j % 2) * 256, 256)
                kv = dot_nt(wa_h, tokA[j // 2, rows]) + dot_nt(wb_h, tokB[j // 2, rows])
                kv = kv.astype(jnp.bfloat16)
                sc = dot_nn(qs[pl.ds(j * 64, 64), cols], kv[:128]) * SCALE
                sc = jnp.exp(sc - jnp.max(sc, axis=1, keepdims=True))
                w = (sc / jnp.sum(sc, axis=1, keepdims=True)).astype(jnp.bfloat16)
                parts.append(dot_nt(w, kv[128:]))
            comb = pltpu.roll(jnp.concatenate(parts, axis=0), 255, 0)
            stage[g, :, pl.ds(zh * 128, 128)] = comb.astype(jnp.bfloat16)
        to_next, zero, one, edge = out_copies(g)
        to_next.start()

        @pl.when(k == 0)
        def _():
            zero.start()
            out_ref[pl.ds(64, 64), qcols(g, 0)] = stage[g, pl.ds(0, 64)]
            fix[:, qcols(g, 0)] = stage[g, pl.ds(240, 16)]

        @pl.when(k == 1)
        def _():
            one.start()
            edge.start()
            out_ref[:, qcols(g, 1)] = stage[g, pl.ds(64, 128)]

    pltpu.make_async_copy(q_all.at[pl.ds(0, 64)], q_all.at[pl.ds(0, 64)], osem.at[0]).wait()
    pltpu.make_async_copy(whole_q, whole_q, qsem.at[0]).wait()

    @pl.when(k == 0)
    def _():
        sixty_four = q_all.at[pl.ds(0, 64)]
        sixteen = q_all.at[pl.ds(0, 16)]
        arrived(sixty_four, qsem.at[1])
        arrived(sixty_four, qsem.at[2])
        arrived(whole_q, osem.at[1])
        arrived(sixty_four, s_o.at[0])
        arrived(sixty_four, s_o.at[1])
        arrived(sixty_four, s_o.at[3])
        arrived(sixteen, s_o.at[4])
        first = s == 0

        @pl.when(first)
        def _():
            out_ref[pl.ds(0, 48)] = jnp.zeros((48, 4096), jnp.bfloat16)

        @pl.loop(0, 8)
        def _(g):
            cols = pl.ds(pl.multiple_of(g * 512, 512), 512)
            row = lax.broadcasted_iota(jnp.int32, (16, 512), 0)
            came = out_ref[pl.ds(48, 16), cols].astype(jnp.float32)
            came = jnp.where(first, 0.0, came)
            own = fix[:, cols].astype(jnp.float32)
            out_ref[pl.ds(48, 16), cols] = jnp.where(row == 15, own, came).astype(jnp.bfloat16)

    @pl.when(k == 1)
    def _():
        arrived(q_all.at[pl.ds(0, 64)], osem.at[2])
        arrived(q_all.at[pl.ds(0, 16)], osem.at[3])
        arrived(whole_q, s_o.at[2])

    for t in always:
        t().wait_send()

    @pl.when(act)
    def _():
        for t in if_act:
            t().wait_send()

    @pl.when(jnp.logical_not(act))
    def _():
        for t in if_pas:
            t().wait_send()


def body(queries, encoded, projection, neighbour_shard, neighbour_block):
    bf = jnp.bfloat16
    dma = pltpu.SemaphoreType.DMA
    hbm = pl.BlockSpec(memory_space=pl.ANY)
    smem = pl.BlockSpec(memory_space=pltpu.SMEM)
    out = pl.pallas_call(
        kernel,
        name="spans",
        out_shape=jax.ShapeDtypeStruct((128, 4096), bf),
        in_specs=[hbm, hbm, hbm, smem, smem],
        out_specs=pl.BlockSpec(memory_space=pltpu.VMEM),
        scratch_shapes=[
            pltpu.VMEM((4, 2, 8, 64, LA), bf),
            pltpu.VMEM((4, 2, 8, 64, LB), bf),
            pltpu.VMEM((12, 128, 896), bf),
            pltpu.VMEM((3, 2, 128, LA), bf),
            pltpu.VMEM((3, 2, 128, LB), bf),
            pltpu.VMEM((8, 128, LA), bf),
            pltpu.VMEM((8, 128, LB), bf),
            pltpu.VMEM((2, 512, LA), bf),
            pltpu.VMEM((2, 512, LB), bf),
            pltpu.VMEM((320, 2048), bf),
            pltpu.VMEM((256, 2048), bf),
            pltpu.VMEM((8, 256, 256), bf),
            pltpu.VMEM((16, 4096), bf),
            pltpu.VMEM((8, 128), jnp.int32),
            pltpu.VMEM((4, 8, 128), jnp.int32),
            pltpu.SMEM((4, 8, 128), jnp.int32),
            dma((5,)),
            dma((80,)),
            dma((3,)),
            dma((4,)),
            dma((4,)),
            dma((2, 4)),
            dma((2,)),
            dma((4, 2)),
            dma((8, 2)),
            dma((2,)),
            dma((2, 4, 2)),
            dma((4,)),
            dma((2, 4, 2)),
            dma((2,)),
            dma((5,)),
        ],
        compiler_params=pltpu.CompilerParams(
            collective_id=0, has_side_effects=True, vmem_limit_bytes=48 * 2**20
        ),
        cost_estimate=pl.CostEstimate(flops=8 * 10**9, bytes_accessed=6 * 2**20, transcendentals=10**6),
    )(queries[0], encoded[0, 0], projection.T, neighbour_shard, neighbour_block)
    return out[None]


def solution(mesh):
    placed = (
        P("dp", "seq", None),
        P("dp", "seq", None, None, None),
        P(None, ("dp", "seq")),
        P("dp", "seq", None),
        P("dp", "seq", None),
    )
    return jax.shard_map(
        body, mesh=mesh, in_specs=placed, out_specs=P("dp", "seq", None), check_vma=False
    )
```

time: 234 us -> 122 us (0.52)
  the two profiles are of different devices: /device:TPU:8 before, /device:TPU:2 now
where the time goes in v1:
time: 122 us
  Pallas kernels  116 us (95%)
  local copies, waits for them, and re-layouts  6.15 us (5%)
    pallas_call x1, Pallas kernels, body(): pl.pallas_call(kernel, name='spans', out_shape=jax.ShapeDtypeStruct((128,...  116 us
    unnamed x11, local copies, waits for them, and re-layouts  6.15 us

profile of v1, /device:TPU:2, one launch (start us, length us, event | category | flops | bytes accessed | tf_op | source)
XLA Modules:
  0.0 122.1 jit_solution(7226017270572904228)
XLA Ops:
  0.0 0.0 copy-start
  0.0 1.8 %copy-done = bf16[1,1,12,128,896]{4,3,2,1,0:T(8,128)(2,1)S(1)} copy-done((bf16[1,1,12,128,896]{4,3,2,1,0:T(8,128)(2,1)S(1)}, bf16[1,1,12,128,896]{4,3,2,1,0:T(8,128)(2,1)}, u32[]{:S(2)}) %copy-start) | copy-done | bytes 2752536
  1.8 0.0 copy-start.1
  1.8 1.2 %copy-done.1 = bf16[1,128,4096]{2,1,0:T(8,128)(2,1)S(1)} copy-done((bf16[1,128,4096]{2,1,0:T(8,128)(2,1)S(1)}, bf16[1,128,4096]{2,1,0:T(8,128)(2,1)}, u32[]{:S(2)}) %copy-start.1) | copy-done | bytes 1048600
  3.0 0.0 copy-start.2
  3.0 0.8 copy-done.2
  3.8 0.0 copy-start.3
  3.8 0.7 copy-done.3
  4.5 0.0 copy-start.4
  4.5 0.7 copy-done.4
  5.2 116.0 %spans.1 = bf16[128,4096]{1,0:T(8,128)(2,1)S(1)} custom-call(bf16[128,4096]{1,0:T(8,128)(2,1)S(1)} %bitcast.6, bf16[12,128,896]{2,1,0:T(8,128)(2,1)S(1)} %bitcast.5, bf16[32,896]{1,0:T(8,128)(2,1)S(1)} %bitcast.7, s32[1,2,2]{2,1,0:T(2,128)S(1)} %copy-done.3, s32[1,2,2]{2,1,0:T(2,128)S(1)} %copy-done.4), custom_call_target="tpu_custom_call" | custom-call | flops 8000000000 | bytes 6291456 | tf_op jit(solution)/shard_map/spans/pallas_call | solution.py:460
  121.1 1.0 copy.7
Async XLA Ops:
  0.0 1.8 %copy-start = (bf16[1,1,12,128,896]{4,3,2,1,0:T(8,128)(2,1)S(1)}, bf16[1,1,12,128,896]{4,3,2,1,0:T(8,128)(2,1)}, u32[]{:S(2)}) copy-start(bf16[1,1,12,128,896]{4,3,2,1,0:T(8,128)(2,1)} %param.6) | copy-start | bytes 8257540
  1.8 1.2 %copy-start.1 = (bf16[1,128,4096]{2,1,0:T(8,128)(2,1)S(1)}, bf16[1,128,4096]{2,1,0:T(8,128)(2,1)}, u32[]{:S(2)}) copy-start(bf16[1,128,4096]{2,1,0:T(8,128)(2,1)} %param.5) | copy-start | bytes 3145732
  3.0 0.8 copy-start.2
  3.8 0.7 copy-start.3
  4.5 0.7 copy-start.4

commit v2 on v0

v2 whole, which is shorter than its diff:
```python
import math

import jax
import jax.numpy as jnp
from jax import lax
from jax.experimental import pallas as pl
from jax.experimental.pallas import tpu as pltpu
from jax.sharding import PartitionSpec as P

MESH = pl.DeviceIdType.MESH
HD = 128
CH = 64
LA = 384
LB = 512
SCALE = 1.0 / math.sqrt(HD)


def dot_nt(a, b):
    return lax.dot_general(a, b, (((1,), (1,)), ((), ())), preferred_element_type=jnp.float32)


def dot_nn(a, b):
    return lax.dot_general(a, b, (((1,), (0,)), ((), ())), preferred_element_type=jnp.float32)


XS = {0: 0, 3: 1, 1: 2, 2: 3}
XR = (0, 3, 1, 2)
ZS = {0: 0, 1: 1, 7: 2, 2: 3, 6: 4, 3: 5, 5: 6, 4: 7}
DO_P1 = DO_P2 = DO_TOK = DO_Q = DO_OUT = DO_MATH = True


def kernel(
    q_ref, enc_hbm, wt_ref, sh_hbm, bl_hbm, out_ref,
    WA, WB, KV, enc, packA, packB, recvA, recvB, tokA, tokB, q_all, qs, stage, fix, idx_out, idx_in, idx_smem,
    sh_ref, bl_ref,
    lsem, ssem, qsem, osem, s_idx, s_tok, s_sib, s_p1x, s_p2z, s_p1y, s_p1z, s_p2x, s_p2y, s_q, s_o,
):
    x = lax.axis_index("dp")
    s = lax.axis_index("seq")
    y = lax.div(s, 16)
    z = lax.rem(lax.div(s, 2), 8)
    k = lax.rem(s, 2)
    yy = lax.div(y, 2)
    cs = lax.rem(y, 2)
    act = cs == k
    pas = jnp.logical_not(act)

    def dev(dx=0, dy=0, dz=0, core=None):
        core = k if core is None else core
        return (
            lax.rem(x + dx + 4, 4),
            lax.rem(y + dy + 4, 4) * 16 + lax.rem(z + dz + 8, 8) * 2 + core,
        )

    def chip_along(step, core):
        return (x, lax.rem(lax.div(s, 2) + step + 32, 32) * 2 + core)

    sib = dev(core=1 - k)
    counter = [0]

    def remote(src, dst, rsem, to):
        n = counter[0]
        counter[0] += 1

        def build():
            return pltpu.make_async_remote_copy(
                src_ref=src, dst_ref=dst, send_sem=ssem.at[n], recv_sem=rsem, device_id=to, device_id_type=MESH
            )

        return build

    def arrived(dst, rsem):
        pltpu.make_async_copy(dst, dst, rsem).wait()

    sh_cp = pltpu.make_async_copy(sh_hbm, sh_ref, lsem.at[5])
    bl_cp = pltpu.make_async_copy(bl_hbm, bl_ref, lsem.at[6])
    sh_cp.start()
    bl_cp.start()
    enc_cp = pltpu.make_async_copy(enc_hbm, enc, lsem.at[0])
    enc_cp.start()

    barrier = pltpu.get_barrier_semaphore()
    partners = [sib]
    for c in (0, 1):
        partners += [dev(dx=d, core=c) for d in (1, 2, 3)]
        partners += [dev(dz=d, core=c) for d in range(1, 8)]
        partners += [chip_along(1, c), chip_along(-1, c)]
    partners += [dev(dy=d) for d in (1, 2, 3)]
    for p in partners:
        pl.semaphore_signal(barrier, inc=1, device_id=p, device_id_type=MESH)

    lane = lax.broadcasted_iota(jnp.int32, (8, 128), 1)
    sh_cp.wait()
    bl_cp.wait()
    own_sh = [sh_ref[0, e // 2, e % 2] for e in range(4)]
    own_bl = [bl_ref[0, e // 2, e % 2] for e in range(4)]
    codes = jnp.zeros((8, 128), jnp.int32)
    for e in range(4):
        codes = jnp.where(lane == e, own_sh[e], codes)
        codes = jnp.where(lane == 4 + e, own_bl[e], codes)
    idx_out[...] = codes
    pl.semaphore_wait(barrier, len(partners))

    always, if_act, if_pas = [], [], []

    for d in (1, 2, 3):
        always.append(remote(idx_out, idx_in.at[x], s_idx.at[d], dev(dx=d)))
        always[-1]().start()

    wa = wt_ref.at[:, pl.ds(0, LA)]
    wb = wt_ref.at[:, pl.ds(LA, LB)]
    half = pl.ds(pl.multiple_of(k * 32, 32), 32)
    other = pl.ds(pl.multiple_of((1 - k) * 32, 32), 32)
    ownA = lambda: pltpu.make_async_copy(wa, WA.at[0, yy, 0, half], lsem.at[1])
    ownB = lambda: pltpu.make_async_copy(wb, WB.at[0, yy, 0, half], lsem.at[2])
    sibA = remote(wa, WA.at[0, yy, 0, half], s_p1x.at[0, k], sib)
    sibB = remote(wb, WB.at[0, yy, 0, half], s_p2z.at[0, k], sib)
    if_pas += [sibA, sibB]

    @pl.when(act)
    def _():
        ownA().start()
        ownB().start()

    @pl.when(pas)
    def _():
        sibA().start()
        sibB().start()

    for d in (4, 3, 5, 2, 6, 1, 7):
        always.append(remote(wb, WB.at[0, yy, ZS[8 - d], half], s_p2z.at[d, k], dev(dz=d, core=cs)))
        always[-1]().start()
    for d in (2, 1, 3):
        always.append(remote(wa, WA.at[XS[4 - d], yy, 0, half], s_p1x.at[d, k], dev(dx=d, core=cs)))
        always[-1]().start()

    local_rows = pl.ds(pl.multiple_of(k * 128, 128), 128)

    def qcols(g, core):
        return pl.ds(pl.multiple_of(g * 512 + core * 256, 256), 256)

    def gcols(g):
        return pl.ds(pl.multiple_of(g * 256, 256), 256)

    def q_copies(g):
        loc = pltpu.make_async_copy(q_ref.at[:, qcols(g, k)], q_all.at[local_rows, gcols(g)], lsem.at[4])
        to_sib = pltpu.make_async_remote_copy(
            src_ref=q_ref.at[:, qcols(g, 1 - k)], dst_ref=q_all.at[local_rows, gcols(g)],
            send_sem=qsem.at[0], recv_sem=s_q.at[0], device_id=sib, device_id_type=MESH,
        )
        back = [
            pltpu.make_async_remote_copy(
                src_ref=q_ref.at[pl.ds(0, 64), qcols(g, c)], dst_ref=q_all.at[pl.ds(256, 64), gcols(g)],
                send_sem=qsem.at[1 + c], recv_sem=s_q.at[1], device_id=chip_along(-1, c), device_id_type=MESH,
            )
            for c in (0, 1)
        ]
        return loc, to_sib, back

    if DO_Q:
        @pl.loop(0, 8)
        def _(g):
            loc, to_sib, back = q_copies(g)
            loc.start()
            to_sib.start()

            @pl.when(k == 0)
            def _():
                back[0].start()
                back[1].start()

    enc_cp.wait()

    def wanted(sh, bl):
        m = [v == x for v in sh]
        first = jnp.where(m[0], bl[0], jnp.where(m[1], bl[1], jnp.where(m[2], bl[2], bl[3])))
        last = jnp.where(m[3], bl[3], jnp.where(m[2], bl[2], jnp.where(m[1], bl[1], bl[0])))
        return first, last

    to_smem = {}
    for d in (1, 3, 2):
        src = lax.rem(x + d, 4)
        arrived(idx_in.at[src], s_idx.at[4 - d])
        to_smem[d] = pltpu.make_async_copy(idx_in.at[src], idx_smem.at[src], lsem.at[6 + d])
        to_smem[d].start()
    tokB_sends = []
    for d in (1, 3, 2):
        src = lax.rem(x + d, 4)
        to_smem[d].wait()
        pair = wanted([idx_smem[src, 0, e] for e in range(4)], [idx_smem[src, 0, 4 + e] for e in range(4)])
        for i in range(2):
            block = enc[pair[i]]
            packA[d - 1, i] = block[:, :LA]
            packB[d - 1, i] = block[:, LA:]
        mine = pl.ds(x * 2, 2)
        if DO_TOK:
            always.append(remote(packA.at[d - 1], recvA.at[mine], s_tok.at[0, d], dev(dx=d)))
            always[-1]().start()
            tokB_sends.append(remote(packB.at[d - 1], recvB.at[mine], s_tok.at[1, d], dev(dx=d)))
    pair = wanted(own_sh, own_bl)
    for i in range(2):
        block = enc[pair[i]]
        recvA[x * 2 + i] = block[:, :LA]
        recvB[x * 2 + i] = block[:, LA:]

    p1y = [remote(WA.at[:, yy, 0], WA.at[:, yy, 0], s_p1y.at[yy], dev(dy=d)) for d in (1, 3, 2)]
    if_act += p1y

    def zstep(direction, step, part):
        have, there = (step - 1, step) if direction else ((9 - step) % 8, 8 - step)
        return remote(
            WA.at[:, part, ZS[have]], WA.at[:, part, ZS[there]], s_p1z.at[direction, step - 1, part],
            dev(dz=-1 if direction else 1),
        )

    def zwait(direction, step, part):
        arrived(WA.at[:, part, ZS[step if direction else 8 - step]], s_p1z.at[direction, step - 1, part])

    z_own = [zstep(i, 1, yy) for i in (0, 1)]
    z_far = [zstep(i, 1, 1 - yy) for i in (0, 1)]
    z_next = {st: [(i, p, zstep(i, st, p)) for p in (0, 1) for i in (0, 1)] for st in (2, 3)}
    z_next[4] = [(0, 0, zstep(0, 4, 0)), (1, 1, zstep(1, 4, 1))]
    always += z_own + z_far + [t for st in (2, 3, 4) for _, _, t in z_next[st]]

    def z_forward(st):
        if not DO_P1:
            return
        waited = set()
        for i, p, t in z_next[st]:
            zwait(i, st - 1, p)
            waited.add((i, p))
            t().start()
        for i in (0, 1):
            for p in (0, 1):
                if (i, p) not in waited:
                    zwait(i, st - 1, p)

    p2x = {d: remote(WB.at[0, yy], WB.at[XS[4 - d], yy], s_p2x.at[d], dev(dx=d)) for d in (1, 3, 2)}
    if_act += list(p2x.values())

    def ysend(direction, d, piece, part):
        ref = WB.at[XS[d], part, pl.ds(4 * piece, 4)]
        return remote(ref, ref, s_p2y.at[direction, d, piece], dev(dy=-1 if direction else 1))

    below, above = lax.div(lax.rem(y + 3, 4), 2), lax.div(lax.rem(y + 1, 4), 2)

    def ywait(direction, d, piece):
        part = jnp.where(act, 1 - yy, above if direction else below)
        arrived(WB.at[XS[d], part, pl.ds(4 * piece, 4)], s_p2y.at[direction, d, piece])

    y_act = {d: [ysend(0, d, 0, yy), ysend(1, d, 1, yy), ysend(0, d, 1, yy), ysend(1, d, 0, yy)] for d in range(4)}
    y_pas = {d: [ysend(0, d, 0, below), ysend(1, d, 1, above)] for d in range(4)}
    for d in range(4):
        if_act += y_act[d]
        if_pas += y_pas[d]

    def y_forward(d):
        if not DO_P2:
            return
        ywait(0, d, 0)
        y_pas[d][0]().start()
        ywait(1, d, 1)
        y_pas[d][1]().start()
        ywait(0, d, 1)
        ywait(1, d, 0)

    @pl.when(act)
    def _():
        ownA().wait()
        arrived(WA.at[0, yy, 0, other], s_p1x.at[0, 1 - k])
        for d in (1, 2, 3):
            for c in (0, 1):
                arrived(WA.at[XS[4 - d], yy, 0, pl.ds(c * 32, 32)], s_p1x.at[d, c])
        if DO_P1:
            for t in p1y + z_own:
                t().start()
        ownB().wait()
        arrived(WB.at[0, yy, 0, other], s_p2z.at[0, 1 - k])
        for d in range(1, 8):
            for c in (0, 1):
                arrived(WB.at[0, yy, ZS[8 - d], pl.ds(c * 32, 32)], s_p2z.at[d, c])
        if DO_P2:
            for t in [p2x[1], p2x[3]] + y_act[0]:
                t().start()
        if DO_P1:
            arrived(WA.at[:, 1 - yy, 0], s_p1y.at[1 - yy])
            for t in z_far:
                t().start()

    if DO_P1:
        @pl.when(pas)
        def _():
            for part in (0, 1):
                arrived(WA.at[:, part, 0], s_p1y.at[part])
            for t in z_own + z_far:
                t().start()

    if DO_TOK:
        for t in tokB_sends:
            always.append(t)
            t().start()

    whole_q = q_all.at[pl.ds(0, 128)]
    if DO_Q:
        pltpu.make_async_copy(q_ref.at[:, pl.ds(0, 2048)], whole_q, lsem.at[4]).wait()
        arrived(whole_q, s_q.at[0])
        arrived(q_all.at[pl.ds(256, 64)], s_q.at[1])

        @pl.loop(0, 8)
        def _(g):
            rows = q_all[pl.ds(48, 272), gcols(g)].astype(jnp.float32)
            qs[:, gcols(g)] = pltpu.roll(rows, 1, 0)[16:].astype(jnp.bfloat16)

    @pl.when(pas)
    def _():
        y_forward(0)

    z_forward(2)

    if DO_P2:
        @pl.when(act)
        def _():
            for d in (1, 3):
                arrived(WB.at[XS[4 - d], yy], s_p2x.at[d])
                for t in y_act[4 - d]:
                    t().start()
            p2x[2]().start()

    half_tok = []
    rank = [jnp.int32(0)]
    for e in range(1, 4):
        same = own_sh[e] == own_sh[0]
        for f in range(1, e):
            same = jnp.logical_or(same, own_sh[e] == own_sh[f])
        rank.append(jnp.where(same, 1, 0))

    def take_tokens(which):
        recv, tok = ((recvA, tokA), (recvB, tokB))[which]
        if DO_TOK:
            for d in (1, 2, 3):
                arrived(recv.at[pl.ds(lax.rem(x + 4 - d, 4) * 2, 2)], s_tok.at[which, d])
        for e in range(4):
            tok[k, pl.ds(e * 128, 128)] = recv[own_sh[e] * 2 + rank[e]]
        half_tok.append(remote(tok.at[k], tok.at[k], s_sib.at[which], sib))
        half_tok[-1]().start()

    take_tokens(0)

    @pl.when(pas)
    def _():
        y_forward(3)

    z_forward(3)
    take_tokens(1)

    def project(x0, x1, z0, z1):
        if not DO_MATH:
            return
        rows = (x1 - x0) * 2 * (z1 - z0) * 64
        a = WA[x0:x1, :, z0:z1].reshape(rows, LA)
        b = WB[x0:x1, :, z0:z1].reshape(rows, LB)
        for j in range(4):
            at = pl.ds((j % 2) * 256, 256)
            kv = dot_nt(a, tokA[j // 2, at]) + dot_nt(b, tokB[j // 2, at])
            KV[x0:x1, :, z0:z1, :, j * 256 : j * 256 + 256] = kv.astype(jnp.bfloat16).reshape(
                x1 - x0, 2, z1 - z0, 64, 256
            )

    def plane_of(zabs):
        d = lax.rem(zabs - z + 8, 8)
        return jnp.where(d <= 4, jnp.maximum(2 * d - 1, 0), 16 - 2 * d)

    def attend(xs, zh):
        xa = lax.rem(x + XR[xs], 4)
        if not DO_MATH:
            for part in (0, 1):
                stage[xs * 2 + part, :, pl.ds(pl.multiple_of(zh * 128, 128), 128)] = qs[:, 0:128]
            return
        planes = [plane_of(zh * 4 + i) for i in range(4)]
        units = [(part, j) for part in (0, 1) for j in range(4)]
        scores = []
        for part, j in units:
            cols = pl.ds(pl.multiple_of((xa * 2 + part) * 256 + zh * 128, 128), 128)
            at = slice(j * 256, j * 256 + 256)
            keys = jnp.concatenate([KV[xs, part, planes[0], :, at], KV[xs, part, planes[1], :, at]], axis=0)
            scores.append(dot_nn(qs[j * 64 : j * 64 + 64, cols], keys))
        weights = []
        for sc in scores:
            sc = sc * SCALE
            sc = jnp.exp(sc - jnp.max(sc, axis=1, keepdims=True))
            weights.append((sc * (1.0 / jnp.sum(sc, axis=1, keepdims=True))).astype(jnp.bfloat16))
        parts = []
        for (part, j), w in zip(units, weights):
            at = slice(j * 256, j * 256 + 256)
            values = jnp.concatenate([KV[xs, part, planes[2], :, at], KV[xs, part, planes[3], :, at]], axis=0)
            parts.append(dot_nt(w, values))
        for part in (0, 1):
            comb = pltpu.roll(jnp.concatenate(parts[part * 4 : part * 4 + 4], axis=0), 255, 0)
            stage[xs * 2 + part, :, pl.ds(pl.multiple_of(zh * 128, 128), 128)] = comb.astype(jnp.bfloat16)

    def send_out(xs):
        xa = lax.rem(x + XR[xs], 4)
        for part in (0, 1):
            g = xa * 2 + part
            st = stage.at[xs * 2 + part]
            cols = qcols(g, k)

            def to(src, dst, n, target):
                return pltpu.make_async_remote_copy(
                    src_ref=src, dst_ref=dst, send_sem=osem.at[n], recv_sem=s_o.at[n + 1 if n else k],
                    device_id=target, device_id_type=MESH,
                )

            if DO_OUT:
                to(st.at[pl.ds(192, 64)], out_ref.at[pl.ds(0, 64), cols], 0, chip_along(1, 0)).start()

            @pl.when(k == 0)
            def _():
                if DO_OUT:
                    to(st.at[pl.ds(64, 128)], out_ref.at[:, cols], 1, sib).start()
                out_ref[pl.ds(64, 64), qcols(g, 0)] = st[pl.ds(0, 64)]
                fix[:, qcols(g, 0)] = st[pl.ds(240, 16)]

            @pl.when(k == 1)
            def _():
                if DO_OUT:
                    to(st.at[pl.ds(0, 64)], out_ref.at[pl.ds(64, 64), cols], 2, sib).start()
                    to(st.at[pl.ds(240, 16)], fix.at[:, cols], 3, sib).start()
                out_ref[:, qcols(g, 1)] = st[pl.ds(64, 128)]

    near = lax.div(z, 4)
    arrived(tokA.at[1 - k], s_sib.at[0])
    arrived(tokB.at[1 - k], s_sib.at[1])

    def y_here(d):
        if DO_P2:
            ywait(0, d, 0)
            ywait(1, d, 1)

    @pl.when(act)
    def _():
        y_here(0)

    project(0, 1, 0, 5)

    @pl.when(act)
    def _():
        y_here(3)

    project(1, 2, 0, 5)
    z_forward(4)
    project(0, 2, 5, 7)

    @pl.when(act)
    def _():
        if DO_P2:
            arrived(WB.at[XS[2], yy], s_p2x.at[2])
            for t in y_act[2]:
                t().start()
        y_here(1)

    @pl.when(pas)
    def _():
        y_forward(1)

    project(2, 3, 0, 7)
    attend(0, near)
    attend(1, near)
    attend(2, near)

    @pl.when(pas)
    def _():
        y_forward(2)

    if DO_P1:
        zwait(0, 4, 0)
        zwait(1, 4, 1)
    project(0, 3, 7, 8)
    for xs in range(3):
        attend(xs, 1 - near)
        send_out(xs)

    @pl.when(act)
    def _():
        y_here(2)

    project(3, 4, 0, 8)
    attend(3, near)
    attend(3, 1 - near)
    send_out(3)

    always += half_tok
    sixty_four = q_all.at[pl.ds(0, 64)]
    sixteen = q_all.at[pl.ds(0, 16)]
    if DO_Q:
        arrived(whole_q, qsem.at[0])

        @pl.when(k == 0)
        def _():
            arrived(sixty_four, qsem.at[1])
            arrived(sixty_four, qsem.at[2])

    if DO_OUT:
        arrived(sixty_four, osem.at[0])

        @pl.when(k == 0)
        def _():
            arrived(whole_q, osem.at[1])
            arrived(sixty_four, s_o.at[0])
            arrived(sixty_four, s_o.at[1])
            arrived(sixty_four, s_o.at[3])
            arrived(sixteen, s_o.at[4])
            first = s == 0

            @pl.when(first)
            def _():
                out_ref[pl.ds(0, 48)] = jnp.zeros((48, 4096), jnp.bfloat16)

            @pl.loop(0, 8)
            def _(g):
                cols = pl.ds(pl.multiple_of(g * 512, 512), 512)
                row = lax.broadcasted_iota(jnp.int32, (16, 512), 0)
                came = out_ref[pl.ds(48, 16), cols].astype(jnp.float32)
                came = jnp.where(first, 0.0, came)
                own = fix[:, cols].astype(jnp.float32)
                out_ref[pl.ds(48, 16), cols] = jnp.where(row == 15, own, came).astype(jnp.bfloat16)

        @pl.when(k == 1)
        def _():
            arrived(sixty_four, osem.at[2])
            arrived(sixteen, osem.at[3])
            arrived(whole_q, s_o.at[2])

    skip = set()
    if not DO_P1:
        skip |= set(p1y + z_own + z_far + [t for st in (2, 3, 4) for _, _, t in z_next[st]])
    if not DO_P2:
        skip |= set(list(p2x.values()) + [t for d in range(4) for t in y_act[d] + y_pas[d]])
    for t in always:
        if t not in skip:
            t().wait_send()

    @pl.when(act)
    def _():
        for t in if_act:
            if t not in skip:
                t().wait_send()

    @pl.when(pas)
    def _():
        for t in if_pas:
            if t not in skip:
                t().wait_send()


def body(queries, encoded, projection, neighbour_shard, neighbour_block):
    bf = jnp.bfloat16
    dma = pltpu.SemaphoreType.DMA
    hbm = pl.BlockSpec(memory_space=pl.ANY)
    out = pl.pallas_call(
        kernel,
        name="spans",
        out_shape=jax.ShapeDtypeStruct((128, 4096), bf),
        in_specs=[hbm] * 5,
        out_specs=pl.BlockSpec(memory_space=pltpu.VMEM),
        scratch_shapes=[
            pltpu.VMEM((4, 2, 8, 64, LA), bf),
            pltpu.VMEM((4, 2, 8, 64, LB), bf),
            pltpu.VMEM((4, 2, 8, 64, 1024), bf),
            pltpu.VMEM((12, 128, 896), bf),
            pltpu.VMEM((3, 2, 128, LA), bf),
            pltpu.VMEM((3, 2, 128, LB), bf),
            pltpu.VMEM((8, 128, LA), bf),
            pltpu.VMEM((8, 128, LB), bf),
            pltpu.VMEM((2, 512, LA), bf),
            pltpu.VMEM((2, 512, LB), bf),
            pltpu.VMEM((320, 2048), bf),
            pltpu.VMEM((256, 2048), bf),
            pltpu.VMEM((8, 256, 256), bf),
            pltpu.VMEM((16, 4096), bf),
            pltpu.VMEM((8, 128), jnp.int32),
            pltpu.VMEM((4, 8, 128), jnp.int32),
            pltpu.SMEM((4, 8, 128), jnp.int32),
            pltpu.SMEM((1, 2, 2), jnp.int32),
            pltpu.SMEM((1, 2, 2), jnp.int32),
            dma((10,)),
            dma((80,)),
            dma((3,)),
            dma((4,)),
            dma((4,)),
            dma((2, 4)),
            dma((2,)),
            dma((4, 2)),
            dma((8, 2)),
            dma((2,)),
            dma((2, 4, 2)),
            dma((4,)),
            dma((2, 4, 2)),
            dma((2,)),
            dma((5,)),
        ],
        compiler_params=pltpu.CompilerParams(
            collective_id=0, has_side_effects=True, vmem_limit_bytes=60 * 2**20
        ),
        cost_estimate=pl.CostEstimate(flops=8 * 10**9, bytes_accessed=6 * 2**20, transcendentals=10**6),
    )(queries[0], encoded[0, 0], projection.T, neighbour_shard, neighbour_block)
    return out[None]


def solution(mesh):
    placed = (
        P("dp", "seq", None),
        P("dp", "seq", None, None, None),
        P(None, ("dp", "seq")),
        P("dp", "seq", None),
        P("dp", "seq", None),
    )
    return jax.shard_map(
        body, mesh=mesh, in_specs=placed, out_specs=P("dp", "seq", None), check_vma=False
    )
```

time: 234 us -> 82 us (0.35)
  waiting for transfers between devices: 105 us -> 0 us
  Pallas kernels: 0 us -> 79.5 us
  local copies, waits for them, and re-layouts: 43.9 us -> 2.29 us
  matrix products: 35.4 us -> 0 us
  blocking collectives: 17.4 us -> 0 us
  between operations: 13.6 us -> 0.01 us
  starting transfers between devices: 9.93 us -> 0 us
  other arithmetic: 7.76 us -> 0 us
    pallas_call x0 -> x1, Pallas kernels: none -> 79.5 us  [body(): pl.pallas_call(kernel, name='spans', out_shape=jax.ShapeDtypeStruct((128,...]
    all_gather x1 -> x0, waiting for transfers between devices: 77.8 us -> none  [body(): lax.all_gather(projection, ('dp', 'seq'), axis=1, tiled=True)]
    dot_general x3 -> x0, matrix products: 35.4 us -> none  [the longest x1 16.1 us: attend_blocks(): jnp.einsum('chij,cjhd->cihd', weights, head_split[:, :, :, 1], preferred_...]
    slice x5 -> x0, local copies, waits for them, and re-layouts: 19.8 us -> none  [the longest x1 19.4 us: attend_blocks(): head_split[:, :, :, 0]]
    all_gather x2 -> x0, blocking collectives: 17.4 us -> none  [the longest x1 10.1 us: body(): lax.all_gather(neighbour_shard, 'dp', axis=0, tiled=True)]
    ppermute x2 -> x0, waiting for transfers between devices: 16.9 us -> none  [passed_along(): lax.ppermute(value, axis, [(source, source + steps) for source in range(i...]
    another operation x1 -> x0, local copies, waits for them, and re-layouts: 14.3 us -> none  [attend_blocks(): head_split = key_value.reshape(blocks, key_value.shape[1], groups, 2, HD)]
    all_to_all x1 -> x0, waiting for transfers between devices: 9.43 us -> none  [body(): lax.all_to_all(packed, 'dp', split_axis=0, concat_axis=0, tiled=True)]
  transfers between devices with their start and end apart: 4 -> 0, of which waited for: 4 -> 0; matrix products, arithmetic and copies ran while one was open for 5% -> 0% of each run, Pallas kernels for 0% -> 0%
where the time goes in v2:
time: 82 us; the launch traced here: 81.8 us
  Pallas kernels  79.5 us (97%)
  local copies, waits for them, and re-layouts  2.29 us (3%)
    pallas_call x1, Pallas kernels, body(): pl.pallas_call(kernel, name='spans', out_shape=jax.ShapeDtypeStruct((128,...  79.5 us
    unnamed x1, local copies, waits for them, and re-layouts  2.29 us

profile of v2, /device:TPU:8, one launch (start us, length us, event | category | flops | bytes accessed | tf_op | source)
XLA Modules:
  0.0 81.8 jit_solution(577544177596087825)
XLA Ops:
  0.0 79.5 %spans.1 = bf16[128,4096]{1,0:T(8,128)(2,1)} custom-call(bf16[128,4096]{1,0:T(8,128)(2,1)} %bitcast.6, bf16[12,128,896]{2,1,0:T(8,128)(2,1)} %bitcast.5, bf16[32,896]{1,0:T(8,128)(2,1)} %bitcast.7, s32[1,2,2]{2,1,0:T(2,128)} %sh_hbm.1, s32[1,2,2]{2,1,0:T(2,128)} %bl_hbm.1), custom_call_target="tpu_custom_call" | custom-call | flops 8000000000 | bytes 6291456 | tf_op jit(solution)/shard_map/spans/pallas_call | solution.py:560
  79.5 2.3 %copy.7 = bf16[1,128,4096]{2,1,0:T(8,128)(2,1)} copy(bf16[1,128,4096]{2,1,0:T(8,128)(2,1)} %bitcast.4) | data formatting | bytes 2097152

commit v3 on v2

v3 whole, which is shorter than its diff:
```python
import math

import jax
import jax.numpy as jnp
from jax import lax
from jax.experimental import pallas as pl
from jax.experimental.pallas import tpu as pltpu
from jax.sharding import PartitionSpec as P

MESH = pl.DeviceIdType.MESH
HD = 128
CH = 64
LA = 256
LB = 512
LD = 128
SCALE = 1.0 / math.sqrt(HD)


def dot_nt(a, b):
    return lax.dot_general(a, b, (((1,), (1,)), ((), ())), preferred_element_type=jnp.float32)


def dot_nn(a, b):
    return lax.dot_general(a, b, (((1,), (0,)), ((), ())), preferred_element_type=jnp.float32)


XS = {0: 0, 3: 1, 1: 2, 2: 3}
XR = (0, 3, 1, 2)
ZS = {0: 0, 1: 1, 7: 2, 2: 3, 6: 4, 3: 5, 5: 6, 4: 7}
DO_P1 = DO_P2 = DO_TOK = DO_Q = DO_OUT = DO_MATH = True


def kernel(
    q_ref, enc_hbm, wt_ref, sh_hbm, bl_hbm, out_ref,
    W, KV, enc, pack, recv, tok, q_all, qs, stage, fix, idx_out, idx_in, idx_smem,
    sh_ref, bl_ref,
    lsem, ssem, qsem, osem, s_idx, s_tok, s_sib, s_wx, s_p1y, s_p1z, s_p2z, s_p2y, s_dy, s_dz, s_dx, s_q, s_o,
):
    x = lax.axis_index("dp")
    s = lax.axis_index("seq")
    y = lax.div(s, 16)
    z = lax.rem(lax.div(s, 2), 8)
    k = lax.rem(s, 2)
    yy = lax.div(y, 2)
    cs = lax.rem(y, 2)
    act = cs == k
    pas = jnp.logical_not(act)

    def dev(dx=0, dy=0, dz=0, core=None):
        core = k if core is None else core
        return (
            lax.rem(x + dx + 4, 4),
            lax.rem(y + dy + 4, 4) * 16 + lax.rem(z + dz + 8, 8) * 2 + core,
        )

    def chip_along(step, core):
        return (x, lax.rem(lax.div(s, 2) + step + 32, 32) * 2 + core)

    sib = dev(core=1 - k)
    counter = [0]

    def remote(src, dst, rsem, to):
        n = counter[0]
        counter[0] += 1

        def build():
            return pltpu.make_async_remote_copy(
                src_ref=src, dst_ref=dst, send_sem=ssem.at[n], recv_sem=rsem, device_id=to, device_id_type=MESH
            )

        return build

    def arrived(dst, rsem):
        pltpu.make_async_copy(dst, dst, rsem).wait()

    barrier = pltpu.get_barrier_semaphore()
    partners = [sib]
    for c in (0, 1):
        partners += [dev(dx=d, core=c) for d in (1, 2, 3)]
        partners += [chip_along(1, c), chip_along(-1, c)]
        partners += [dev(dy=d, core=c) for d in (1, 2, 3)]
    partners += [dev(dz=d) for d in (1, -1)]
    for p in partners:
        pl.semaphore_signal(barrier, inc=1, device_id=p, device_id_type=MESH)

    sh_cp = pltpu.make_async_copy(sh_hbm, sh_ref, lsem.at[5])
    bl_cp = pltpu.make_async_copy(bl_hbm, bl_ref, lsem.at[6])
    sh_cp.start()
    bl_cp.start()
    enc_cp = pltpu.make_async_copy(enc_hbm, enc, lsem.at[0])
    enc_cp.start()

    lane = lax.broadcasted_iota(jnp.int32, (8, 128), 1)
    sh_cp.wait()
    bl_cp.wait()
    own_sh = [sh_ref[0, e // 2, e % 2] for e in range(4)]
    own_bl = [bl_ref[0, e // 2, e % 2] for e in range(4)]
    codes = jnp.zeros((8, 128), jnp.int32)
    for e in range(4):
        codes = jnp.where(lane == e, own_sh[e], codes)
        codes = jnp.where(lane == 4 + e, own_bl[e], codes)
    idx_out[...] = codes
    pl.semaphore_wait(barrier, len(partners))

    always, if_act, if_pas = [], [], []

    for d in (1, 2, 3):
        always.append(remote(idx_out, idx_in.at[x], s_idx.at[d], dev(dx=d)))
        always[-1]().start()

    half = pl.ds(pl.multiple_of(k * 32, 32), 32)
    other = pl.ds(pl.multiple_of((1 - k) * 32, 32), 32)
    fa, fb, fd, fab = pl.ds(0, LA), pl.ds(LA, LB), pl.ds(LA + LB, LD), pl.ds(0, LA + LB)
    own = lambda: pltpu.make_async_copy(wt_ref, W.at[0, yy, 0, half], lsem.at[1])
    to_sib_w = remote(wt_ref, W.at[0, yy, 0, half], s_wx.at[0, k], sib)
    if_pas.append(to_sib_w)

    @pl.when(act)
    def _():
        own().start()

    @pl.when(pas)
    def _():
        to_sib_w().start()

    for d in (2, 1, 3):
        always.append(
            remote(wt_ref.at[:, fab], W.at[XS[4 - d], yy, 0, half, fab], s_wx.at[d, k], dev(dx=d, core=cs))
        )
        always[-1]().start()
    for d in (2, 1, 3):
        always.append(remote(wt_ref.at[:, fd], W.at[0, yy, 0, half, fd], s_dy.at[d, k], dev(dy=d, core=cs)))
        always[-1]().start()

    local_rows = pl.ds(pl.multiple_of(k * 128, 128), 128)

    def qcols(g, core):
        return pl.ds(pl.multiple_of(g * 512 + core * 256, 256), 256)

    def gcols(g):
        return pl.ds(pl.multiple_of(g * 256, 256), 256)

    def q_copies(g):
        loc = pltpu.make_async_copy(q_ref.at[:, qcols(g, k)], q_all.at[local_rows, gcols(g)], lsem.at[4])
        to_sib = pltpu.make_async_remote_copy(
            src_ref=q_ref.at[:, qcols(g, 1 - k)], dst_ref=q_all.at[local_rows, gcols(g)],
            send_sem=qsem.at[0], recv_sem=s_q.at[0], device_id=sib, device_id_type=MESH,
        )
        back = [
            pltpu.make_async_remote_copy(
                src_ref=q_ref.at[pl.ds(0, 64), qcols(g, c)], dst_ref=q_all.at[pl.ds(256, 64), gcols(g)],
                send_sem=qsem.at[1 + c], recv_sem=s_q.at[1], device_id=chip_along(-1, c), device_id_type=MESH,
            )
            for c in (0, 1)
        ]
        return loc, to_sib, back

    if DO_Q:
        @pl.loop(0, 8)
        def _(g):
            loc, to_sib, back = q_copies(g)
            loc.start()
            to_sib.start()

            @pl.when(k == 0)
            def _():
                back[0].start()
                back[1].start()

    p1y = [remote(W.at[:, yy, 0, :, fa], W.at[:, yy, 0, :, fa], s_p1y.at[yy], dev(dy=d)) for d in (1, 3, 2)]
    if_act += p1y

    def ends_of(direction, step):
        return (ZS[step - 1], ZS[step]) if direction else (ZS[(9 - step) % 8], ZS[8 - step])

    def zstep(direction, step, part):
        have, there = ends_of(direction, step)
        return remote(
            W.at[:, part, have, :, fa], W.at[:, part, there, :, fa], s_p1z.at[direction, step - 1, part],
            dev(dz=-1 if direction else 1),
        )

    def zwait(direction, step, part):
        arrived(W.at[:, part, ends_of(direction, step)[1], :, fa], s_p1z.at[direction, step - 1, part])

    def dstep(direction, step, part):
        have, there = ends_of(direction, step)
        return remote(
            W.at[0, part, have, :, fd], W.at[0, part, there, :, fd], s_dz.at[direction, step - 1, part],
            dev(dz=-1 if direction else 1),
        )

    def dwait(direction, step, part):
        arrived(W.at[0, part, ends_of(direction, step)[1], :, fd], s_dz.at[direction, step - 1, part])

    PIECES = ((0, 3), (3, 5), (5, 7), (7, 8))
    dx = {}
    for i, (z0, z1) in enumerate(PIECES):
        dx[i] = [
            remote(W.at[0, :, z0:z1, :, fd], W.at[XS[4 - d], :, z0:z1, :, fd], s_dx.at[d, i], dev(dx=d))
            for d in (2, 1, 3)
        ]
        always += dx[i]

    def dxsend(i):
        for t in dx[i]:
            t().start()

    def dxwait(i):
        z0, z1 = PIECES[i]
        for d in (1, 3, 2):
            arrived(W.at[XS[4 - d], :, z0:z1, :, fd], s_dx.at[d, i])

    z_own = [zstep(i, 1, yy) for i in (0, 1)] + [dstep(i, 1, yy) for i in (0, 1)]
    z_far = [zstep(i, 1, 1 - yy) for i in (0, 1)] + [dstep(i, 1, 1 - yy) for i in (0, 1)]
    z_next = {st: [(i, p, zstep(i, st, p), dstep(i, st, p)) for p in (0, 1) for i in (0, 1)] for st in (2, 3)}
    z_next[4] = [(0, 0, zstep(0, 4, 0), dstep(0, 4, 0)), (1, 1, zstep(1, 4, 1), dstep(1, 4, 1))]
    always += z_own + z_far + [t for st in (2, 3, 4) for n in z_next[st] for t in n[2:]]

    def z_forward(st):
        if not DO_P1:
            return
        waited = set()
        for i, p, t, u in z_next[st]:
            zwait(i, st - 1, p)
            dwait(i, st - 1, p)
            waited.add((i, p))
            t().start()
            u().start()
        for i in (0, 1):
            for p in (0, 1):
                if (i, p) not in waited:
                    zwait(i, st - 1, p)
                    dwait(i, st - 1, p)
        dxsend(st - 2)

    def columns_of(direction, step):
        return pl.ds(2 * direction, 2) if step == 4 else pl.ds(0, 4)

    def bstep(direction, step):
        have, there = ends_of(direction, step)
        xs = columns_of(direction, step)
        return remote(
            W.at[xs, yy, have, :, fb], W.at[xs, yy, there, :, fb], s_p2z.at[direction, step - 1],
            dev(dz=-1 if direction else 1),
        )

    def bwait(direction, step):
        arrived(W.at[columns_of(direction, step), yy, ends_of(direction, step)[1], :, fb], s_p2z.at[direction, step - 1])

    b_steps = {st: [bstep(i, st) for i in (0, 1)] for st in (1, 2, 3, 4)}
    for st in (1, 2, 3, 4):
        if_act += b_steps[st]

    def ysend(direction, plane, piece, part):
        ref = W.at[pl.ds(2 * piece, 2), part, ZS[plane], :, fb]
        return remote(ref, ref, s_p2y.at[direction, plane, piece], dev(dy=-1 if direction else 1))

    below, above = lax.div(lax.rem(y + 3, 4), 2), lax.div(lax.rem(y + 1, 4), 2)

    def ywait(direction, plane, piece):
        part = jnp.where(act, 1 - yy, above if direction else below)
        arrived(W.at[pl.ds(2 * piece, 2), part, ZS[plane], :, fb], s_p2y.at[direction, plane, piece])

    y_act = {d: [ysend(0, d, 0, yy), ysend(1, d, 1, yy), ysend(0, d, 1, yy), ysend(1, d, 0, yy)] for d in range(8)}
    y_pas = {d: [ysend(0, d, 0, below), ysend(1, d, 1, above)] for d in range(8)}
    for d in range(8):
        if_act += y_act[d]
        if_pas += y_pas[d]

    def b_forward(st):
        if not DO_P2:
            return
        for i in (0, 1):
            bwait(i, st)
            if st < 4:
                b_steps[st + 1][i]().start() if st < 3 or i == 0 else None
        if st == 3:
            b_steps[4][1]().start()
        for plane in (8 - st, st) if st < 4 else (4,):
            for t in y_act[plane]:
                t().start()

    def y_forward(plane):
        if not DO_P2:
            return
        ywait(0, plane, 0)
        y_pas[plane][0]().start()
        ywait(1, plane, 1)
        y_pas[plane][1]().start()

    def y_rest(plane):
        if not DO_P2:
            return
        ywait(0, plane, 1)
        ywait(1, plane, 0)

    def y_here(plane):
        if not DO_P2:
            return
        ywait(0, plane, 0)
        ywait(1, plane, 1)

    @pl.when(act)
    def _():
        own().wait()
        arrived(W.at[0, yy, 0, other], s_wx.at[0, 1 - k])
        for d in (1, 3, 2):
            for c in (0, 1):
                arrived(W.at[XS[4 - d], yy, 0, pl.ds(c * 32, 32), fab], s_wx.at[d, c])
        if DO_P1:
            for t in p1y:
                t().start()
        if DO_P2:
            for t in b_steps[1] + y_act[0]:
                t().start()
        if DO_P1:
            for t in z_own:
                t().start()

    enc_cp.wait()

    def wanted(sh, bl):
        m = [v == x for v in sh]
        first = jnp.where(m[0], bl[0], jnp.where(m[1], bl[1], jnp.where(m[2], bl[2], bl[3])))
        last = jnp.where(m[3], bl[3], jnp.where(m[2], bl[2], jnp.where(m[1], bl[1], bl[0])))
        return first, last

    to_smem = {}
    for d in (1, 3, 2):
        src = lax.rem(x + d, 4)
        arrived(idx_in.at[src], s_idx.at[4 - d])
        to_smem[d] = pltpu.make_async_copy(idx_in.at[src], idx_smem.at[src], lsem.at[6 + d])
        to_smem[d].start()
    for d in (1, 3, 2):
        src = lax.rem(x + d, 4)
        to_smem[d].wait()
        pair = wanted([idx_smem[src, 0, e] for e in range(4)], [idx_smem[src, 0, 4 + e] for e in range(4)])
        for i in range(2):
            pack[d - 1, i] = enc[pair[i]]
        if DO_TOK:
            always.append(remote(pack.at[d - 1], recv.at[pl.ds(x * 2, 2)], s_tok.at[d], dev(dx=d)))
            always[-1]().start()
    pair = wanted(own_sh, own_bl)
    for i in range(2):
        recv[x * 2 + i] = enc[pair[i]]

    if DO_P1:
        @pl.when(act)
        def _():
            arrived(W.at[:, 1 - yy, 0, :, fa], s_p1y.at[1 - yy])
            for c in (0, 1):
                arrived(W.at[0, 1 - yy, 0, pl.ds(c * 32, 32), fd], s_dy.at[2, c])
            for t in z_far:
                t().start()

        @pl.when(pas)
        def _():
            for part in (0, 1):
                arrived(W.at[:, part, 0, :, fa], s_p1y.at[part])
            for c in (0, 1):
                arrived(W.at[0, below, 0, pl.ds(c * 32, 32), fd], s_dy.at[1, c])
                arrived(W.at[0, above, 0, pl.ds(c * 32, 32), fd], s_dy.at[3, c])
            for t in z_own + z_far:
                t().start()

    @pl.when(act)
    def _():
        b_forward(1)

    @pl.when(pas)
    def _():
        y_forward(0)

    z_forward(2)

    @pl.when(act)
    def _():
        b_forward(2)

    @pl.when(pas)
    def _():
        y_forward(7)
        y_forward(1)

    half_tok = []
    rank = [jnp.int32(0)]
    for e in range(1, 4):
        same = own_sh[e] == own_sh[0]
        for f in range(1, e):
            same = jnp.logical_or(same, own_sh[e] == own_sh[f])
        rank.append(jnp.where(same, 1, 0))

    @pl.when(act)
    def _():
        b_forward(3)

    z_forward(3)

    @pl.when(pas)
    def _():
        y_forward(6)


    if DO_TOK:
        for d in (1, 2, 3):
            arrived(recv.at[pl.ds(lax.rem(x + 4 - d, 4) * 2, 2)], s_tok.at[d])
    for e in range(4):
        tok[k, pl.ds(e * 128, 128)] = recv[own_sh[e] * 2 + rank[e]]
    half_tok.append(remote(tok.at[k], tok.at[k], s_sib.at[0], sib))
    half_tok[-1]().start()

    def project(z0, z1):
        if not DO_MATH:
            return
        rows = 8 * (z1 - z0) * 64
        a = W[:, :, z0:z1].reshape(rows, LA + LB + LD)
        for j in range(4):
            kv = dot_nt(a, tok[j // 2, pl.ds((j % 2) * 256, 256)])
            KV[:, :, z0:z1, :, j * 256 : j * 256 + 256] = kv.astype(jnp.bfloat16).reshape(4, 2, z1 - z0, 64, 256)

    def plane_of(zabs):
        d = lax.rem(zabs - z + 8, 8)
        return jnp.where(d <= 4, jnp.maximum(2 * d - 1, 0), 16 - 2 * d)

    def attend(xs, zh):
        xa = lax.rem(x + XR[xs], 4)
        if not DO_MATH:
            for part in (0, 1):
                stage[xs * 2 + part, :, pl.ds(pl.multiple_of(zh * 128, 128), 128)] = qs[:, 0:128]
            return
        planes = [plane_of(zh * 4 + i) for i in range(4)]
        units = [(part, j) for part in (0, 1) for j in range(4)]
        scores = []
        for part, j in units:
            cols = pl.ds(pl.multiple_of((xa * 2 + part) * 256 + zh * 128, 128), 128)
            at = slice(j * 256, j * 256 + 256)
            keys = jnp.concatenate([KV[xs, part, planes[0], :, at], KV[xs, part, planes[1], :, at]], axis=0)
            scores.append(dot_nn(qs[j * 64 : j * 64 + 64, cols], keys))
        weights = []
        for sc in scores:
            sc = sc * SCALE
            sc = jnp.exp(sc - jnp.max(sc, axis=1, keepdims=True))
            weights.append((sc * (1.0 / jnp.sum(sc, axis=1, keepdims=True))).astype(jnp.bfloat16))
        parts = []
        for (part, j), w in zip(units, weights):
            at = slice(j * 256, j * 256 + 256)
            values = jnp.concatenate([KV[xs, part, planes[2], :, at], KV[xs, part, planes[3], :, at]], axis=0)
            parts.append(dot_nt(w, values))
        for part in (0, 1):
            comb = pltpu.roll(jnp.concatenate(parts[part * 4 : part * 4 + 4], axis=0), 255, 0)
            stage[xs * 2 + part, :, pl.ds(pl.multiple_of(zh * 128, 128), 128)] = comb.astype(jnp.bfloat16)

    def send_out(xs, zh):
        xa = lax.rem(x + XR[xs], 4)
        lanes = pl.ds(pl.multiple_of(zh * 128, 128), 128)
        for part in (0, 1):
            st = stage.at[xs * 2 + part]
            cols = pl.ds(pl.multiple_of((xa * 2 + part) * 512 + k * 256 + zh * 128, 128), 128)

            def to(src, dst, n, target):
                return pltpu.make_async_remote_copy(
                    src_ref=src, dst_ref=dst, send_sem=osem.at[n], recv_sem=s_o.at[n + 1 if n else k],
                    device_id=target, device_id_type=MESH,
                )

            if DO_OUT:
                to(st.at[pl.ds(192, 64), lanes], out_ref.at[pl.ds(0, 64), cols], 0, chip_along(1, 0)).start()

            @pl.when(k == 0)
            def _():
                if DO_OUT:
                    to(st.at[pl.ds(64, 128), lanes], out_ref.at[:, cols], 1, sib).start()
                out_ref[pl.ds(64, 64), cols] = st[pl.ds(0, 64), lanes]
                fix[:, cols] = st[pl.ds(240, 16), lanes]

            @pl.when(k == 1)
            def _():
                if DO_OUT:
                    to(st.at[pl.ds(0, 64), lanes], out_ref.at[pl.ds(64, 64), cols], 2, sib).start()
                    to(st.at[pl.ds(240, 16), lanes], fix.at[:, cols], 3, sib).start()
                out_ref[:, cols] = st[pl.ds(64, 128), lanes]

    near = lax.div(z, 4)

    whole_q = q_all.at[pl.ds(0, 128)]
    if DO_Q:
        pltpu.make_async_copy(q_ref.at[:, pl.ds(0, 2048)], whole_q, lsem.at[4]).wait()
        arrived(whole_q, s_q.at[0])
        arrived(q_all.at[pl.ds(256, 64)], s_q.at[1])

        @pl.loop(0, 8)
        def _(g):
            rows = q_all[pl.ds(48, 272), gcols(g)].astype(jnp.float32)
            qs[:, gcols(g)] = pltpu.roll(rows, 1, 0)[16:].astype(jnp.bfloat16)

    arrived(tok.at[1 - k], s_sib.at[0])

    def here(*planes):
        @pl.when(act)
        def _():
            for plane in planes:
                y_here(plane)

        @pl.when(pas)
        def _():
            for plane in planes:
                y_rest(plane)

    def forward_b(plane):
        @pl.when(pas)
        def _():
            y_forward(plane)

    dxwait(0)
    here(0)
    project(0, 1)

    @pl.when(act)
    def _():
        b_forward(4)

    forward_b(2)
    here(7, 1)
    project(1, 3)
    z_forward(4)
    forward_b(5)
    here(6, 2)
    dxwait(1)
    project(3, 5)
    forward_b(3)
    here(5, 3)
    dxwait(2)
    project(5, 7)
    forward_b(4)
    for xs in range(2):
        attend(xs, near)
        send_out(xs, near)

    if DO_P1:
        for i in (0, 1):
            zwait(i, 4, i)
            dwait(i, 4, i)
        dxsend(3)

    for xs in range(2, 4):
        attend(xs, near)
        send_out(xs, near)

    @pl.when(act)
    def _():
        y_here(4)

    @pl.when(pas)
    def _():
        y_rest(4)

    dxwait(3)
    project(7, 8)

    skip = set()
    for t in always + half_tok:
        if t not in skip:
            t().wait_send()

    @pl.when(act)
    def _():
        for t in if_act:
            if t not in skip:
                t().wait_send()

    @pl.when(pas)
    def _():
        for t in if_pas:
            if t not in skip:
                t().wait_send()

    if DO_Q:
        arrived(whole_q, qsem.at[0])

        @pl.when(k == 0)
        def _():
            arrived(q_all.at[pl.ds(0, 64)], qsem.at[1])
            arrived(q_all.at[pl.ds(0, 64)], qsem.at[2])

    for xs in range(4):
        attend(xs, 1 - near)
        send_out(xs, 1 - near)

    sixty_four = q_all.at[pl.ds(0, 64)]
    sixteen = q_all.at[pl.ds(0, 16)]
    if DO_OUT:
        arrived(sixty_four, osem.at[0])

        @pl.when(k == 0)
        def _():
            arrived(whole_q, osem.at[1])
            arrived(sixty_four, s_o.at[0])
            arrived(sixty_four, s_o.at[1])
            arrived(sixty_four, s_o.at[3])
            arrived(sixteen, s_o.at[4])
            first = s == 0

            @pl.when(first)
            def _():
                out_ref[pl.ds(0, 48)] = jnp.zeros((48, 4096), jnp.bfloat16)

            @pl.loop(0, 8)
            def _(g):
                cols = pl.ds(pl.multiple_of(g * 512, 512), 512)
                row = lax.broadcasted_iota(jnp.int32, (16, 512), 0)
                came = out_ref[pl.ds(48, 16), cols].astype(jnp.float32)
                came = jnp.where(first, 0.0, came)
                own = fix[:, cols].astype(jnp.float32)
                out_ref[pl.ds(48, 16), cols] = jnp.where(row == 15, own, came).astype(jnp.bfloat16)

        @pl.when(k == 1)
        def _():
            arrived(sixty_four, osem.at[2])
            arrived(sixteen, osem.at[3])
            arrived(whole_q, s_o.at[2])


def body(queries, encoded, projection, neighbour_shard, neighbour_block):
    bf = jnp.bfloat16
    dma = pltpu.SemaphoreType.DMA
    hbm = pl.BlockSpec(memory_space=pl.ANY)
    out = pl.pallas_call(
        kernel,
        name="spans",
        out_shape=jax.ShapeDtypeStruct((128, 4096), bf),
        in_specs=[hbm] * 5,
        out_specs=pl.BlockSpec(memory_space=pltpu.VMEM),
        scratch_shapes=[
            pltpu.VMEM((4, 2, 8, 64, LA + LB + LD), bf),
            pltpu.VMEM((4, 2, 8, 64, 1024), bf),
            pltpu.VMEM((12, 128, 896), bf),
            pltpu.VMEM((3, 2, 128, 896), bf),
            pltpu.VMEM((8, 128, 896), bf),
            pltpu.VMEM((2, 512, 896), bf),
            pltpu.VMEM((320, 2048), bf),
            pltpu.VMEM((256, 2048), bf),
            pltpu.VMEM((8, 256, 256), bf),
            pltpu.VMEM((16, 4096), bf),
            pltpu.VMEM((8, 128), jnp.int32),
            pltpu.VMEM((4, 8, 128), jnp.int32),
            pltpu.SMEM((4, 8, 128), jnp.int32),
            pltpu.SMEM((1, 2, 2), jnp.int32),
            pltpu.SMEM((1, 2, 2), jnp.int32),
            dma((10,)),
            dma((130,)),
            dma((3,)),
            dma((4,)),
            dma((4,)),
            dma((4,)),
            dma((1,)),
            dma((4, 2)),
            dma((2,)),
            dma((2, 4, 2)),
            dma((2, 4)),
            dma((2, 8, 2)),
            dma((4, 2)),
            dma((2, 4, 2)),
            dma((4, 4)),
            dma((2,)),
            dma((5,)),
        ],
        compiler_params=pltpu.CompilerParams(
            collective_id=0, has_side_effects=True, vmem_limit_bytes=60 * 2**20
        ),
        cost_estimate=pl.CostEstimate(flops=8 * 10**9, bytes_accessed=6 * 2**20, transcendentals=10**6),
    )(queries[0], encoded[0, 0], projection.T, neighbour_shard, neighbour_block)
    return out[None]


def solution(mesh):
    placed = (
        P("dp", "seq", None),
        P("dp", "seq", None, None, None),
        P(None, ("dp", "seq")),
        P("dp", "seq", None),
        P("dp", "seq", None),
    )
    return jax.shard_map(
        body, mesh=mesh, in_specs=placed, out_specs=P("dp", "seq", None), check_vma=False
    )
```

time: 82 us -> 77.5 us (0.945)
  Pallas kernels: 79.5 us -> 74.3 us
    pallas_call x1, Pallas kernels: 79.5 us -> 74.3 us  [body(): pl.pallas_call(kernel, name='spans', out_shape=jax.ShapeDtypeStruct((128,...]
where the time goes in v3:
time: 77.5 us; the launch traced here: 76.6 us
  Pallas kernels  74.3 us (96%)
  local copies, waits for them, and re-layouts  2.29 us (3%)
    pallas_call x1, Pallas kernels, body(): pl.pallas_call(kernel, name='spans', out_shape=jax.ShapeDtypeStruct((128,...  74.3 us
    unnamed x1, local copies, waits for them, and re-layouts  2.29 us

profile of v3, /device:TPU:8, one launch (start us, length us, event | category | flops | bytes accessed | tf_op | source)
XLA Modules:
  0.0 76.6 jit_solution(5661477532166424164)
XLA Ops:
  0.0 74.3 %spans.1 = bf16[128,4096]{1,0:T(8,128)(2,1)} custom-call(bf16[128,4096]{1,0:T(8,128)(2,1)} %bitcast.6, bf16[12,128,896]{2,1,0:T(8,128)(2,1)} %bitcast.5, bf16[32,896]{1,0:T(8,128)(2,1)} %bitcast.7, s32[1,2,2]{2,1,0:T(2,128)} %sh_hbm.1, s32[1,2,2]{2,1,0:T(2,128)} %bl_hbm.1), custom_call_target="tpu_custom_call" | custom-call | flops 8000000000 | bytes 6291456 | tf_op jit(solution)/shard_map/spans/pallas_call | solution.py:628
  74.3 2.3 %copy.7 = bf16[1,128,4096]{2,1,0:T(8,128)(2,1)} copy(bf16[1,128,4096]{2,1,0:T(8,128)(2,1)} %bitcast.4) | data formatting | bytes 2097152

commit v4 on v3

--- a/solution.py
+++ b/solution.py
@@ -27,7 +27,6 @@
 XS = {0: 0, 3: 1, 1: 2, 2: 3}
 XR = (0, 3, 1, 2)
 ZS = {0: 0, 1: 1, 7: 2, 2: 3, 6: 4, 3: 5, 5: 6, 4: 7}
-DO_P1 = DO_P2 = DO_TOK = DO_Q = DO_OUT = DO_MATH = True
 
 
 def kernel(
@@ -155,17 +154,16 @@
         ]
         return loc, to_sib, back
 
-    if DO_Q:
-        @pl.loop(0, 8)
-        def _(g):
-            loc, to_sib, back = q_copies(g)
-            loc.start()
-            to_sib.start()
-
-            @pl.when(k == 0)
-            def _():
-                back[0].start()
-                back[1].start()
+    @pl.loop(0, 8)
+    def _(g):
+        loc, to_sib, back = q_copies(g)
+        loc.start()
+        to_sib.start()
+
+        @pl.when(k == 0)
+        def _():
+            back[0].start()
+            back[1].start()
 
     p1y = [remote(W.at[:, yy, 0, :, fa], W.at[:, yy, 0, :, fa], s_p1y.at[yy], dev(dy=d)) for d in (1, 3, 2)]
     if_act += p1y
@@ -218,8 +216,6 @@
     always += z_own + z_far + [t for st in (2, 3, 4) for n in z_next[st] for t in n[2:]]
 
     def z_forward(st):
-        if not DO_P1:
-            return
         waited = set()
         for i, p, t, u in z_next[st]:
             zwait(i, st - 1, p)
@@ -269,8 +265,6 @@
         if_pas += y_pas[d]
 
     def b_forward(st):
-        if not DO_P2:
-            return
         for i in (0, 1):
             bwait(i, st)
             if st < 4:
@@ -282,22 +276,16 @@
                 t().start()
 
     def y_forward(plane):
-        if not DO_P2:
-            return
         ywait(0, plane, 0)
         y_pas[plane][0]().start()
         ywait(1, plane, 1)
         y_pas[plane][1]().start()
 
     def y_rest(plane):
-        if not DO_P2:
-            return
         ywait(0, plane, 1)
         ywait(1, plane, 0)
 
     def y_here(plane):
-        if not DO_P2:
-            return
         ywait(0, plane, 0)
         ywait(1, plane, 1)
 
@@ -308,15 +296,12 @@
         for d in (1, 3, 2):
             for c in (0, 1):
                 arrived(W.at[XS[4 - d], yy, 0, pl.ds(c * 32, 32), fab], s_wx.at[d, c])
-        if DO_P1:
-            for t in p1y:
-                t().start()
-        if DO_P2:
-            for t in b_steps[1] + y_act[0]:
-                t().start()
-        if DO_P1:
-            for t in z_own:
-                t().start()
+        for t in p1y:
+            t().start()
+        for t in b_steps[1] + y_act[0]:
+            t().start()
+        for t in z_own:
+            t().start()
 
     enc_cp.wait()
 
@@ -332,37 +317,35 @@
         arrived(idx_in.at[src], s_idx.at[4 - d])
         to_smem[d] = pltpu.make_async_copy(idx_in.at[src], idx_smem.at[src], lsem.at[6 + d])
         to_smem[d].start()
-    for d in (1, 3, 2):
+    for d in (2, 1, 3):
         src = lax.rem(x + d, 4)
         to_smem[d].wait()
         pair = wanted([idx_smem[src, 0, e] for e in range(4)], [idx_smem[src, 0, 4 + e] for e in range(4)])
         for i in range(2):
             pack[d - 1, i] = enc[pair[i]]
-        if DO_TOK:
-            always.append(remote(pack.at[d - 1], recv.at[pl.ds(x * 2, 2)], s_tok.at[d], dev(dx=d)))
-            always[-1]().start()
+        always.append(remote(pack.at[d - 1], recv.at[pl.ds(x * 2, 2)], s_tok.at[d], dev(dx=d)))
+        always[-1]().start()
     pair = wanted(own_sh, own_bl)
     for i in range(2):
         recv[x * 2 + i] = enc[pair[i]]
 
-    if DO_P1:
-        @pl.when(act)
-        def _():
-            arrived(W.at[:, 1 - yy, 0, :, fa], s_p1y.at[1 - yy])
-            for c in (0, 1):
-                arrived(W.at[0, 1 - yy, 0, pl.ds(c * 32, 32), fd], s_dy.at[2, c])
-            for t in z_far:
-                t().start()
-
-        @pl.when(pas)
-        def _():
-            for part in (0, 1):
-                arrived(W.at[:, part, 0, :, fa], s_p1y.at[part])
-            for c in (0, 1):
-                arrived(W.at[0, below, 0, pl.ds(c * 32, 32), fd], s_dy.at[1, c])
-                arrived(W.at[0, above, 0, pl.ds(c * 32, 32), fd], s_dy.at[3, c])
-            for t in z_own + z_far:
-                t().start()
+    @pl.when(act)
+    def _():
+        arrived(W.at[:, 1 - yy, 0, :, fa], s_p1y.at[1 - yy])
+        for c in (0, 1):
+            arrived(W.at[0, 1 - yy, 0, pl.ds(c * 32, 32), fd], s_dy.at[2, c])
+        for t in z_far:
+            t().start()
+
+    @pl.when(pas)
+    def _():
+        for part in (0, 1):
+            arrived(W.at[:, part, 0, :, fa], s_p1y.at[part])
+        for c in (0, 1):
+            arrived(W.at[0, below, 0, pl.ds(c * 32, 32), fd], s_dy.at[1, c])
+            arrived(W.at[0, above, 0, pl.ds(c * 32, 32), fd], s_dy.at[3, c])
+        for t in z_own + z_far:
+            t().start()
 
     @pl.when(act)
     def _():
@@ -402,17 +385,14 @@
         y_forward(6)
 
 
-    if DO_TOK:
-        for d in (1, 2, 3):
-            arrived(recv.at[pl.ds(lax.rem(x + 4 - d, 4) * 2, 2)], s_tok.at[d])
+    for d in (1, 2, 3):
+        arrived(recv.at[pl.ds(lax.rem(x + 4 - d, 4) * 2, 2)], s_tok.at[d])
     for e in range(4):
         tok[k, pl.ds(e * 128, 128)] = recv[own_sh[e] * 2 + rank[e]]
     half_tok.append(remote(tok.at[k], tok.at[k], s_sib.at[0], sib))
     half_tok[-1]().start()
 
     def project(z0, z1):
-        if not DO_MATH:
-            return
         rows = 8 * (z1 - z0) * 64
         a = W[:, :, z0:z1].reshape(rows, LA + LB + LD)
         for j in range(4):
@@ -423,16 +403,13 @@
         d = lax.rem(zabs - z + 8, 8)
         return jnp.where(d <= 4, jnp.maximum(2 * d - 1, 0), 16 - 2 * d)
 
-    def attend(xs, zh):
-        xa = lax.rem(x + XR[xs], 4)
-        if not DO_MATH:
-            for part in (0, 1):
-                stage[xs * 2 + part, :, pl.ds(pl.multiple_of(zh * 128, 128), 128)] = qs[:, 0:128]
-            return
+    def attend(columns, zh):
+        lanes = pl.ds(pl.multiple_of(zh * 128, 128), 128)
         planes = [plane_of(zh * 4 + i) for i in range(4)]
-        units = [(part, j) for part in (0, 1) for j in range(4)]
+        units = [(xs, part, j) for xs in columns for part in (0, 1) for j in range(4)]
         scores = []
-        for part, j in units:
+        for xs, part, j in units:
+            xa = lax.rem(x + XR[xs], 4)
             cols = pl.ds(pl.multiple_of((xa * 2 + part) * 256 + zh * 128, 128), 128)
             at = slice(j * 256, j * 256 + 256)
             keys = jnp.concatenate([KV[xs, part, planes[0], :, at], KV[xs, part, planes[1], :, at]], axis=0)
@@ -443,13 +420,17 @@
             sc = jnp.exp(sc - jnp.max(sc, axis=1, keepdims=True))
             weights.append((sc * (1.0 / jnp.sum(sc, axis=1, keepdims=True))).astype(jnp.bfloat16))
         parts = []
-        for (part, j), w in zip(units, weights):
+        for (xs, part, j), w in zip(units, weights):
             at = slice(j * 256, j * 256 + 256)
             values = jnp.concatenate([KV[xs, part, planes[2], :, at], KV[xs, part, planes[3], :, at]], axis=0)
             parts.append(dot_nt(w, values))
-        for part in (0, 1):
-            comb = pltpu.roll(jnp.concatenate(parts[part * 4 : part * 4 + 4], axis=0), 255, 0)
-            stage[xs * 2 + part, :, pl.ds(pl.multiple_of(zh * 128, 128), 128)] = comb.astype(jnp.bfloat16)
+        for n, xs in enumerate(columns):
+            for part in (0, 1):
+                first = (n * 2 + part) * 4
+                comb = pltpu.roll(jnp.concatenate(parts[first : first + 4], axis=0), 255, 0)
+                stage[xs * 2 + part, :, lanes] = comb.astype(jnp.bfloat16)
+        for xs in columns:
+            send_out(xs, zh)
 
     def send_out(xs, zh):
         xa = lax.rem(x + XR[xs], 4)
@@ -464,35 +445,31 @@
                     device_id=target, device_id_type=MESH,
                 )
 
-            if DO_OUT:
-                to(st.at[pl.ds(192, 64), lanes], out_ref.at[pl.ds(0, 64), cols], 0, chip_along(1, 0)).start()
+            to(st.at[pl.ds(192, 64), lanes], out_ref.at[pl.ds(0, 64), cols], 0, chip_along(1, 0)).start()
 
             @pl.when(k == 0)
             def _():
-                if DO_OUT:
-                    to(st.at[pl.ds(64, 128), lanes], out_ref.at[:, cols], 1, sib).start()
+                to(st.at[pl.ds(64, 128), lanes], out_ref.at[:, cols], 1, sib).start()
                 out_ref[pl.ds(64, 64), cols] = st[pl.ds(0, 64), lanes]
                 fix[:, cols] = st[pl.ds(240, 16), lanes]
 
             @pl.when(k == 1)
             def _():
-                if DO_OUT:
-                    to(st.at[pl.ds(0, 64), lanes], out_ref.at[pl.ds(64, 64), cols], 2, sib).start()
-                    to(st.at[pl.ds(240, 16), lanes], fix.at[:, cols], 3, sib).start()
+                to(st.at[pl.ds(0, 64), lanes], out_ref.at[pl.ds(64, 64), cols], 2, sib).start()
+                to(st.at[pl.ds(240, 16), lanes], fix.at[:, cols], 3, sib).start()
                 out_ref[:, cols] = st[pl.ds(64, 128), lanes]
 
     near = lax.div(z, 4)
 
     whole_q = q_all.at[pl.ds(0, 128)]
-    if DO_Q:
-        pltpu.make_async_copy(q_ref.at[:, pl.ds(0, 2048)], whole_q, lsem.at[4]).wait()
-        arrived(whole_q, s_q.at[0])
-        arrived(q_all.at[pl.ds(256, 64)], s_q.at[1])
-
-        @pl.loop(0, 8)
-        def _(g):
-            rows = q_all[pl.ds(48, 272), gcols(g)].astype(jnp.float32)
-            qs[:, gcols(g)] = pltpu.roll(rows, 1, 0)[16:].astype(jnp.bfloat16)
+    pltpu.make_async_copy(q_ref.at[:, pl.ds(0, 2048)], whole_q, lsem.at[4]).wait()
+    arrived(whole_q, s_q.at[0])
+    arrived(q_all.at[pl.ds(256, 64)], s_q.at[1])
+
+    @pl.loop(0, 8)
+    def _(g):
+        rows = q_all[pl.ds(48, 272), gcols(g)].astype(jnp.float32)
+        qs[:, gcols(g)] = pltpu.roll(rows, 1, 0)[16:].astype(jnp.bfloat16)
 
     arrived(tok.at[1 - k], s_sib.at[0])
 
@@ -533,19 +510,14 @@
     dxwait(2)
     project(5, 7)
     forward_b(4)
-    for xs in range(2):
-        attend(xs, near)
-        send_out(xs, near)
-
-    if DO_P1:
-        for i in (0, 1):
-            zwait(i, 4, i)
-            dwait(i, 4, i)
-        dxsend(3)
-
-    for xs in range(2, 4):
-        attend(xs, near)
-        send_out(xs, near)
+    attend((0, 1), near)
+
+    for i in (0, 1):
+        zwait(i, 4, i)
+        dwait(i, 4, i)
+    dxsend(3)
+
+    attend((2, 3), near)
 
     @pl.when(act)
     def _():
@@ -558,67 +530,59 @@
     dxwait(3)
     project(7, 8)
 
-    skip = set()
     for t in always + half_tok:
-        if t not in skip:
+        t().wait_send()
+
+    @pl.when(act)
+    def _():
+        for t in if_act:
             t().wait_send()
 
-    @pl.when(act)
-    def _():
-        for t in if_act:
-            if t not in skip:
-                t().wait_send()
-
     @pl.when(pas)
     def _():
         for t in if_pas:
-            if t not in skip:
-                t().wait_send()
-
-    if DO_Q:
-        arrived(whole_q, qsem.at[0])
-
-        @pl.when(k == 0)
-        def _():
-            arrived(q_all.at[pl.ds(0, 64)], qsem.at[1])
-            arrived(q_all.at[pl.ds(0, 64)], qsem.at[2])
-
-    for xs in range(4):
-        attend(xs, 1 - near)
-        send_out(xs, 1 - near)
+            t().wait_send()
+
+    arrived(whole_q, qsem.at[0])
+
+    @pl.when(k == 0)
+    def _():
+        arrived(q_all.at[pl.ds(0, 64)], qsem.at[1])
+        arrived(q_all.at[pl.ds(0, 64)], qsem.at[2])
+
+    attend((0, 1, 2, 3), 1 - near)
 
     sixty_four = q_all.at[pl.ds(0, 64)]
     sixteen = q_all.at[pl.ds(0, 16)]
-    if DO_OUT:
-        arrived(sixty_four, osem.at[0])
-
-        @pl.when(k == 0)
+    arrived(sixty_four, osem.at[0])
+
+    @pl.when(k == 0)
+    def _():
+        arrived(whole_q, osem.at[1])
+        arrived(sixty_four, s_o.at[0])
+        arrived(sixty_four, s_o.at[1])
+        arrived(sixty_four, s_o.at[3])
+        arrived(sixteen, s_o.at[4])
+        first = s == 0
+
+        @pl.when(first)
         def _():
-            arrived(whole_q, osem.at[1])
-            arrived(sixty_four, s_o.at[0])
-            arrived(sixty_four, s_o.at[1])
-            arrived(sixty_four, s_o.at[3])
-            arrived(sixteen, s_o.at[4])
-            first = s == 0
-
-            @pl.when(first)
-            def _():
-                out_ref[pl.ds(0, 48)] = jnp.zeros((48, 4096), jnp.bfloat16)
-
-            @pl.loop(0, 8)
-            def _(g):
-                cols = pl.ds(pl.multiple_of(g * 512, 512), 512)
-                row = lax.broadcasted_iota(jnp.int32, (16, 512), 0)
-                came = out_ref[pl.ds(48, 16), cols].astype(jnp.float32)
-                came = jnp.where(first, 0.0, came)
-                own = fix[:, cols].astype(jnp.float32)
-                out_ref[pl.ds(48, 16), cols] = jnp.where(row == 15, own, came).astype(jnp.bfloat16)
-
-        @pl.when(k == 1)
-        def _():
-            arrived(sixty_four, osem.at[2])
-            arrived(sixteen, osem.at[3])
-            arrived(whole_q, s_o.at[2])
+            out_ref[pl.ds(0, 48)] = jnp.zeros((48, 4096), jnp.bfloat16)
+
+        @pl.loop(0, 8)
+        def _(g):
+            cols = pl.ds(pl.multiple_of(g * 512, 512), 512)
+            row = lax.broadcasted_iota(jnp.int32, (16, 512), 0)
+            came = out_ref[pl.ds(48, 16), cols].astype(jnp.float32)
+            came = jnp.where(first, 0.0, came)
+            own = fix[:, cols].astype(jnp.float32)
+            out_ref[pl.ds(48, 16), cols] = jnp.where(row == 15, own, came).astype(jnp.bfloat16)
+
+    @pl.when(k == 1)
+    def _():
+        arrived(sixty_four, osem.at[2])
+        arrived(sixteen, osem.at[3])
+        arrived(whole_q, s_o.at[2])
 
 
 def body(queries, encoded, projection, neighbour_shard, neighbour_block):

time: 77.5 us -> 77 us (level)
  no operation moved by 1% of the time
where the time goes in v4:
time: 77 us; the launch traced here: 76.2 us
  Pallas kernels  73.9 us (96%)
  local copies, waits for them, and re-layouts  2.29 us (3%)
    pallas_call x1, Pallas kernels, body(): pl.pallas_call(kernel, name='spans', out_shape=jax.ShapeDtypeStruct((128,...  73.9 us
    unnamed x1, local copies, waits for them, and re-layouts  2.29 us

profile of v4, /device:TPU:8, one launch (start us, length us, event | category | flops | bytes accessed | tf_op | source)
XLA Modules:
  0.0 76.2 jit_solution(9110250796133776141)
XLA Ops:
  0.0 73.9 %spans.1 = bf16[128,4096]{1,0:T(8,128)(2,1)} custom-call(bf16[128,4096]{1,0:T(8,128)(2,1)} %bitcast.6, bf16[12,128,896]{2,1,0:T(8,128)(2,1)} %bitcast.5, bf16[32,896]{1,0:T(8,128)(2,1)} %bitcast.7, s32[1,2,2]{2,1,0:T(2,128)} %sh_hbm.1, s32[1,2,2]{2,1,0:T(2,128)} %bl_hbm.1), custom_call_target="tpu_custom_call" | custom-call | flops 8000000000 | bytes 6291456 | tf_op jit(solution)/shard_map/spans/pallas_call | solution.py:592
  73.9 2.3 %copy.7 = bf16[1,128,4096]{2,1,0:T(8,128)(2,1)} copy(bf16[1,128,4096]{2,1,0:T(8,128)(2,1)} %bitcast.4) | data formatting | bytes 2097152
